TPU v7x, 128 devices: a whole 4x4x4 slice. The times are simulated.
128 devices in a mesh: rows: 32 (over x_hi, y, z), text: 4 (over x_lo, core).
Axes of the slice: x: 4 (x_hi: 2, x_lo: 2; x = x_hi * 2 + x_lo), y: 4, z: 4, core: 2. Of those that a mesh axis runs over, the one named last changes fastest.
Arguments:
- image_tokens: bfloat16 [32, 512, 2048], P('rows', 'text'), may hold values from -6 to 6
- caption_embed: bfloat16 [32, 32, 4096], P('rows', 'text'), may hold values from -6 to 6
- caption_lengths: int32 [32, 2], P('rows'), may hold values from 5 to 16, as said below
- output_grad: bfloat16 [32, 512, 2048], P('rows', 'text'), may hold values from -6 to 6
- norm_self: bfloat16 [2048], P('rows'), may hold values from 0.5 to 1.5
- norm_cross: bfloat16 [2048], P('rows'), may hold values from 0.5 to 1.5
- norm_feed: bfloat16 [2048], P('rows'), may hold values from 0.5 to 1.5
- self_query: bfloat16 [2048, 2048], P('rows', 'text'), may hold values from -0.125 to 0.125
- self_key: bfloat16 [2048, 2048], P('rows', 'text'), may hold values from -0.125 to 0.125
- self_value: bfloat16 [2048, 2048], P('rows', 'text'), may hold values from -0.125 to 0.125
- self_output: bfloat16 [2048, 2048], P('text', 'rows'), may hold values from -1.5 to 1.5
- cross_query: bfloat16 [2048, 2048], P('rows', 'text'), may hold values from -0.125 to 0.125
- cross_key: bfloat16 [4096, 2048], P('rows', 'text'), may hold values from -0.09375 to 0.09375
- cross_value: bfloat16 [4096, 2048], P('rows', 'text'), may hold values from -0.09375 to 0.09375
- cross_output: bfloat16 [2048, 2048], P('text', 'rows'), may hold values from -0.375 to 0.375
- up_weight: bfloat16 [2048, 8192], P('rows', 'text'), may hold values from -0.125 to 0.125
- down_weight: bfloat16 [8192, 2048], P('text', 'rows'), may hold values from -0.0625 to 0.0625
Outputs:
- layer_output_array: bfloat16 [32, 512, 2048], P('rows', 'text')
- image_grad: float32 [32, 512, 2048], P('rows', 'text')
- caption_grad: float32 [32, 32, 4096], P('rows', 'text')
- norm_self_grad: float32 [2048], P('rows')
- norm_cross_grad: float32 [2048], P('rows')
- norm_feed_grad: float32 [2048], P('rows')
- self_query_grad: float32 [2048, 2048], P('rows', 'text')
- self_key_grad: float32 [2048, 2048], P('rows', 'text')
- self_value_grad: float32 [2048, 2048], P('rows', 'text')
- self_output_grad: float32 [2048, 2048], P('text', 'rows')
- cross_query_grad: float32 [2048, 2048], P('rows', 'text')
- cross_key_grad: float32 [4096, 2048], P('rows', 'text')
- cross_value_grad: float32 [4096, 2048], P('rows', 'text')
- cross_output_grad: float32 [2048, 2048], P('text', 'rows')
- up_grad: float32 [2048, 8192], P('rows', 'text')
- down_grad: float32 [8192, 2048], P('text', 'rows')
Inputs may be any that keep to these rules, and one draw needn't show every extreme that they name: caption_lengths[r, i] counts the live slots of image i's caption; slots at or past it are padding. Some image has 16 live slots and some has 5.
All inputs are finite; a program needn't handle non-finite values.
Results may differ from a plain program's by a relative error of at most 0.029.
Values may be sent and summed in bfloat16 or wider, within the bound.
No kernel may reach another device: no remote copies, remote signals or barrier semaphores. Data moves between devices by JAX's collectives and lax.ppermute only.
A program may use at most 192 MiB of HBM per device.

v0:
```python
import functools

import jax
import jax.numpy as jnp
from jax import lax
from jax.experimental import pallas as pl
from jax.experimental.pallas import tpu as pltpu
from jax.sharding import Mesh, PartitionSpec as P

HEAD = 128
CAP = 16
EPSILON = 1e-05
SCALE = HEAD ** (-0.5)
BF = jnp.bfloat16
F32 = jnp.float32
RING = ("xh", "xl")
PLANE = ("y", "z")
WHOLE = pl.BlockSpec(memory_space=pltpu.VMEM)
HBM = pl.BlockSpec(memory_space=pltpu.MemorySpace.HBM)
ANY = pl.BlockSpec(memory_space=pl.ANY)
SCALAR = pl.BlockSpec(memory_space=pltpu.SMEM)


def shape(dims, dtype=BF):
    return jax.ShapeDtypeStruct(dims, dtype)


def out_of(value):
    return pltpu.with_memory_space_constraint(value, pltpu.MemorySpace.HBM)


def far(dims, dtype=BF):
    return pltpu.MemorySpace.HBM(dims, dtype)


def kernel(body, outs, args, order=(), vmem=12, in_specs=None, out_specs=None, **more):
    order = [out_of(dep) if dep.size >= 2**20 else dep for dep in order]
    n, outer = len(order), body
    if in_specs is None:
        in_specs = [WHOLE] * len(args)
    if out_specs is None:
        out_specs = jax.tree.map(lambda _: WHOLE, outs)
    spec = more.pop("grid_spec", None)
    if n:
        m = len(args)

        def outer(*refs):
            body(*refs[:m], *refs[m + n :])

    specs = dict(in_specs=list(in_specs) + [HBM] * n, out_specs=out_specs)
    if spec is not None:
        scalars, grid, scratch = spec
        specs = dict(
            grid_spec=pltpu.PrefetchScalarGridSpec(
                num_scalar_prefetch=scalars, grid=grid, scratch_shapes=scratch, **specs
            )
        )
    return pl.pallas_call(
        outer,
        out_shape=outs,
        compiler_params=pltpu.CompilerParams(vmem_limit_bytes=vmem * 2**20),
        cost_estimate=pl.CostEstimate(flops=1000, bytes_accessed=1000, transcendentals=0),
        **specs,
        **more,
    )(*args, *order)


def hold_body(value, out):
    pass


def hold(value, order, away=False):
    return kernel(
        hold_body,
        far(value.shape, value.dtype) if away else shape(value.shape, value.dtype),
        (out_of(value) if away else value,),
        order,
        vmem=4,
        in_specs=[ANY],
        out_specs=ANY,
        input_output_aliases={0: 0},
        name="hold",
    )


def dot(a, b, ca, cb, out=F32):
    return lax.dot_general(a, b, (((ca,), (cb,)), ((), ())), preferred_element_type=F32).astype(out)


def px(value, step):
    return lax.ppermute(value, RING, [(i, (i + step) % 4) for i in range(4)])


def pp(value, axis, step):
    return lax.ppermute(value, axis, [(i, (i + step) % 4) for i in range(4)])


def swap(value, axis):
    return lax.ppermute(value, axis, [(0, 1), (1, 0)])


def after(value, dep):
    first = dep[(slice(0, 1),) * dep.ndim].reshape((1,) * value.ndim).astype(F32)
    return (value.astype(F32) + first * 0.0).astype(value.dtype)


def far_of(left, right):
    half = left.shape[0] // 2
    return [px(left[:half], 1), px(right[half:], -1)]


def pick(value, at):
    return lax.dynamic_index_in_dim(value, at & 3, 0, False, allow_negative_indices=False)


def reduce_tokens(keep, other):
    low = [(keep[i].astype(F32) + other[i].astype(F32)).astype(BF) for i in range(1, 4)]
    return [keep[0], other[0], px(low[0], -1), px(low[1], 1), px(low[2], 2)], low


def stats(resid):
    mean = jnp.mean(resid, -1, keepdims=True)
    centered = resid - mean
    inverse = lax.rsqrt(jnp.mean(centered * centered, -1, keepdims=True) + EPSILON)
    return centered * inverse, inverse


def norm_back(scaled, normed, inverse):
    return inverse * (
        scaled
        - jnp.mean(scaled, -1, keepdims=True)
        - normed * jnp.mean(scaled * normed, -1, keepdims=True)
    )


def total_of(refs):
    total = refs[0][...].astype(F32)
    for ref in refs[1:]:
        total = total + ref[...].astype(F32)
    return total


def rows_of(refs, part=slice(None)):
    return jnp.concatenate([ref[part, :] for ref in refs], 0)


def attend_body(first, count, *refs):
    pieces, w_ref = refs[: 2 * count], refs[2 * count]
    qkv_ref, p_ref, o_ref, keep_ref, send_ref = refs[-5:]
    for i in range(count):
        rows = slice(256 * (first + i), 256 * (first + i + 1))
        x = rows_of(pieces[2 * i : 2 * i + 2], slice(0, 128))
        qkv_ref[rows, :] = dot(x, w_ref[:, :768], 1, 0, BF)
        for h in range(2):
            at = h * HEAD
            q = qkv_ref[rows, at : at + HEAD]
            k = qkv_ref[rows, 256 + at : 256 + at + HEAD]
            v = qkv_ref[rows, 512 + at : 512 + at + HEAD]
            s = dot(q, k, 1, 1) * SCALE
            e = jnp.exp(s - jnp.max(s, -1, keepdims=True))
            p = (e / jnp.sum(e, -1, keepdims=True)).astype(BF)
            p_ref[first + i, h] = p
            o_ref[rows, at : at + HEAD] = dot(p, v, 1, 0, BF)
        part = dot(o_ref[rows, :], w_ref[:, 768:1024], 1, 1, BF)
        keep_ref[i] = part[:128]
        send_ref[i] = part[128:]


def attend(first, count, pieces, weights, saved=(), order=()):
    return kernel(
        functools.partial(attend_body, first, count),
        (
            shape((1024, 768)),
            shape((4, 2, 256, 256)),
            shape((1024, 256)),
            shape((count, 128, 2048)),
            shape((count, 128, 2048)),
        ),
        (*pieces, weights, *saved),
        order,
        input_output_aliases={2 * count + 1 + n: n for n in range(3)} if saved else {},
        name="attend",
    )


def attend_back_body(i, ca, cb, qkv_ref, p_ref, w_ref, *refs):
    g_ref, all_ref, keep_ref, send_ref = refs[-4:]
    rows = slice(256 * i, 256 * (i + 1))
    c = rows_of((ca, cb))
    all_ref[rows, :] = c
    go = dot(c, w_ref[:, 768:1024], 1, 0, BF)
    for h in range(2):
        at = h * HEAD
        q = qkv_ref[rows, at : at + HEAD]
        k = qkv_ref[rows, 256 + at : 256 + at + HEAD]
        v = qkv_ref[rows, 512 + at : 512 + at + HEAD]
        low = p_ref[i, h]
        g = go[:, at : at + HEAD]
        g_ref[rows, 512 + at : 512 + at + HEAD] = dot(low, g, 0, 0, BF)
        gp = dot(g, v, 1, 1)
        p = low.astype(F32)
        gs = (p * (gp - jnp.sum(p * gp, -1, keepdims=True))).astype(BF)
        g_ref[rows, at : at + HEAD] = (dot(gs, k, 1, 0) * SCALE).astype(BF)
        g_ref[rows, 256 + at : 256 + at + HEAD] = (dot(gs, q, 0, 0) * SCALE).astype(BF)
    part = dot(g_ref[rows, :], w_ref[:, :768], 1, 1, BF)
    keep_ref[...] = part[:128]
    send_ref[...] = part[128:]


def attend_back(i, ca, cb, weights, qkv, p, saved, order=()):
    more = () if saved is None else saved
    return kernel(
        functools.partial(attend_back_body, i),
        (shape((1024, 768)), shape((1024, 2048)), shape((128, 2048)), shape((128, 2048))),
        (ca, cb, qkv, p, weights, *more),
        order,
        input_output_aliases={5: 0, 6: 1} if more else {},
        name="attend_back",
    )


def feed_body(i, xa, xb, ga, gb, w_ref, *refs):
    act_ref, g_ref, all_ref, keep_ref, send_ref = refs[-5:]
    rows = slice(256 * i, 256 * (i + 1))
    x = rows_of((xa, xb))
    all_ref[rows, :] = x
    final = rows_of((ga, gb), slice(128, 256))
    for at in range(0, 1024, 256):
        u = dot(x, w_ref[:, at : at + 256], 1, 0)
        ga_hidden = dot(final, w_ref[:, 1024 + at : 1280 + at], 1, 0)
        phi = 0.5 + 0.5 * lax.erf(u * 0.5**0.5)
        act_ref[rows, at : at + 256] = (u * phi).astype(BF)
        slope = phi + u * jnp.exp(-0.5 * u * u) * (0.5 / jnp.pi) ** 0.5
        g_ref[rows, at : at + 256] = (ga_hidden * slope).astype(BF)
    part = dot(g_ref[rows, :], w_ref[:, :1024], 1, 1, BF)
    keep_ref[...] = part[:128]
    send_ref[...] = part[128:]


def feed(i, xa, xb, ga, gb, weights, saved, order=()):
    more = () if saved is None else saved
    return kernel(
        functools.partial(feed_body, i),
        (
            shape((1024, 1024)),
            shape((1024, 1024)),
            shape((1024, 2048)),
            shape((128, 2048)),
            shape((128, 2048)),
        ),
        (xa, xb, ga, gb, weights, *more),
        order,
        input_output_aliases={5: 0, 6: 1, 7: 2} if more else {},
        name="feed",
    )


def feed_out_body(act_ref, down_ref, keep_ref, send_ref):
    part = dot(act_ref[...], down_ref[...], 1, 1, BF)
    for i in range(4):
        keep_ref[i] = part[256 * i : 256 * i + 128]
        send_ref[i] = part[256 * i + 128 : 256 * (i + 1)]


def feed_out(act, weights, order=()):
    out = pl.BlockSpec((4, 128, 256), lambda j: (0, 0, j))
    return kernel(
        feed_out_body,
        (far((4, 128, 2048)), far((4, 128, 2048))),
        (out_of(act), out_of(weights)),
        order,
        grid=(8,),
        in_specs=[
            pl.BlockSpec((1024, 1024), lambda j: (0, 0)),
            pl.BlockSpec((256, 1024), lambda j: (j, 1)),
        ],
        out_specs=(out, out),
        name="feed_out",
    )


def feed_grad_body(x, g, act, *refs):
    gm, out = refs[:8], refs[8]
    columns = pl.ds(pl.multiple_of(pl.program_id(0) * 256, 256), 256)
    out[:, :1024] = dot(x[:, columns], g[...], 0, 0, BF)
    out[:, 1024:] = dot(rows_of(gm), act[...], 0, 0, BF)


def feed_grad(x, g, act, pieces, order=()):
    return kernel(
        feed_grad_body,
        far((2048, 2048)),
        (x, g, act, *map(out_of, pieces)),
        order,
        grid=(8,),
        in_specs=[WHOLE] * 3 + [pl.BlockSpec((128, 256), lambda j: (1, j))] * 8,
        out_specs=pl.BlockSpec((256, 2048), lambda j: (j, 0)),
        name="feed_grad",
    )


def more_grad_body(g, c, o, cross, *refs):
    x, out = refs[:8], refs[8]
    start = pl.multiple_of(pl.program_id(0) * 256, 256)
    columns = pl.ds(start, 256)
    out[:, :768] = dot(rows_of(x), g[...], 0, 0, BF)
    out[:, 768:1024] = dot(c[:, columns], o[...], 0, 0, BF)
    out[:, 1024:] = cross[columns, :]


def more_grad(g, c, o, cross, pieces, order=()):
    return kernel(
        more_grad_body,
        far((2048, 1536)),
        (g, c, o, cross, *map(out_of, pieces)),
        order,
        grid=(8,),
        in_specs=[WHOLE] * 4 + [pl.BlockSpec((128, 256), lambda j: (0, j))] * 8,
        out_specs=pl.BlockSpec((256, 1536), lambda j: (j, 0)),
        name="more_grad",
    )


def fold_body(at_ref, kv_ref, w_ref, kv_out, both_ref):
    kv = jnp.sum(kv_ref[...].astype(F32), 0).astype(BF)
    kv_out[...] = kv
    for n in range(4):
        at = n * HEAD
        part = dot(kv[:, at : at + HEAD], w_ref[:, at : at + HEAD], 1, 1, BF)
        for i in range(4):
            away = (i + 4 - at_ref[2]) & 3
            away = jnp.where(away == 0, 0, jnp.where(away == 3, 1, away + 1))
            both_ref[away, n * CAP : (n + 1) * CAP, :] = part[i * CAP : (i + 1) * CAP]


def fold(place, kv, weights, order=()):
    outs = (shape((64, 512)), shape((4, 64, 2048)))
    return kernel(
        fold_body,
        outs,
        (place, kv, out_of(weights)),
        order,
        in_specs=[
            SCALAR,
            pl.BlockSpec((16, 64, 512), lambda j: (0, 0, 0)),
            pl.BlockSpec((2048, 512), lambda j: (0, 2)),
        ],
        out_specs=(
            pl.BlockSpec((64, 512), lambda j: (0, 0)),
            pl.BlockSpec((4, 64, 2048), lambda j: (0, 0, 0)),
        ),
        grid=(1,),
        name="fold",
    )


def unfold_body(at_ref, b0, b1, b2, b3, kv_ref, w_ref, grad_ref, gkv_ref, rows_ref):
    for n in range(4):
        at = n * HEAD
        for away, ref in zip((0, 3, 1, 2), (b0, b1, b2, b3)):
            image = (at_ref[2] + away) & 3
            rows_ref[image] = ref[n * CAP : (n + 1) * CAP, :]
        rows = rows_ref[...].reshape(64, 2048)
        grad_ref[:, at : at + HEAD] = dot(rows, kv_ref[:, at : at + HEAD], 0, 0, BF)
        gkv_ref[:, at : at + HEAD] = dot(rows, w_ref[:, at : at + HEAD], 1, 0, BF)


def unfold(place, back, kv, weights, order=()):
    slot = pl.BlockSpec((64, 2048), lambda j: (0, 0))
    return kernel(
        unfold_body,
        (shape((2048, 512)), shape((64, 512))),
        (place, *back, kv, out_of(weights)),
        order,
        in_specs=[SCALAR]
        + [slot] * 4
        + [
            pl.BlockSpec((64, 512), lambda j: (0, 0)),
            pl.BlockSpec((2048, 512), lambda j: (0, 2)),
        ],
        out_specs=(
            pl.BlockSpec((2048, 512), lambda j: (0, 0)),
            pl.BlockSpec((64, 512), lambda j: (0, 0)),
        ),
        grid=(1,),
        scratch_shapes=[pltpu.VMEM((4, CAP, 2048), BF)],
        name="unfold",
    )


def slots_of(refs, part):
    return jnp.concatenate([ref[i, part, :] for ref in refs for i in range(4)], 0)


def middle_body(length_ref, *refs):
    x, parts, slots = refs[0], refs[1:6], refs[6:8]
    n2_ref, i2_ref, p2_ref, x3_ref, n3_ref, i3_ref = refs[8:]
    x2 = x[...].astype(F32) + total_of(parts)
    normed, inverse = stats(x2)
    low = normed.astype(BF)
    n2_ref[...] = low
    i2_ref[...] = inverse
    m, n = slots_of(slots, slice(0, 32)), slots_of(slots, slice(32, 64))
    s = (dot(m, low, 1, 1) * SCALE).reshape(16, CAP, 128)
    live = lax.broadcasted_iota(jnp.int32, (1, CAP, 1), 1) < length_ref[0]
    s = jnp.where(live, s, -1e30)
    e = jnp.exp(s - jnp.max(s, 1, keepdims=True))
    p = (e / jnp.sum(e, 1, keepdims=True)).reshape(256, 128)
    p2_ref[...] = p
    x3 = x2 + dot(p.astype(BF), n, 0, 0)
    x3_ref[...] = x3
    normed, inverse = stats(x3)
    n3_ref[...] = normed.astype(BF)
    i3_ref[...] = inverse


def middle(length, x, parts, slots, order=()):
    column = shape((128, 1), F32)
    return kernel(
        middle_body,
        (
            shape((128, 2048)),
            column,
            shape((256, 128), F32),
            shape((128, 2048), F32),
            shape((128, 2048)),
            column,
        ),
        (length, x, *parts, *slots),
        order,
        vmem=16,
        in_specs=[SCALAR] + [WHOLE] * 8,
        name="middle",
    )


def middle_back_body(*refs):
    g3, parts, slots = refs[0], refs[1:6], refs[6:8]
    n2, i2, p2, n3, i3 = refs[8:13]
    g1_ref, low_ref, keep_ref, send_ref = refs[13:]
    g2 = g3[...].astype(F32) + norm_back(total_of(parts), n3[...].astype(F32), i3[...])
    c = g2.astype(BF)
    m, n = slots_of(slots, slice(0, 32)), slots_of(slots, slice(32, 64))
    p = p2[...].reshape(16, CAP, 128)
    gp = dot(n, c, 1, 1).reshape(16, CAP, 128)
    gs = (p * (gp - jnp.sum(p * gp, 1, keepdims=True))).reshape(256, 128) * SCALE
    gs = gs.astype(BF)
    g1 = g2 + norm_back(dot(gs, m, 0, 0), n2[...].astype(F32), i2[...])
    g1_ref[...] = g1
    low_ref[...] = g1.astype(BF)
    gm = dot(gs, n2[...], 1, 0, BF)
    gn = dot(p2[...].astype(BF), c, 1, 0, BF)
    for out, at in ((keep_ref, 0), (send_ref, 128)):
        for i in range(4):
            rows = slice(at + 32 * i, at + 32 * (i + 1))
            out[i, :32, :] = gm[rows]
            out[i, 32:, :] = gn[rows]


def middle_back(g3, parts, slots, n2, i2, p2, n3, i3, order=()):
    slot = shape((4, 64, 2048))
    outs = (shape((128, 2048), F32), shape((128, 2048)), slot, slot)
    args = (g3, *parts, *slots, n2, i2, p2, n3, i3)
    return kernel(middle_back_body, outs, args, order, vmem=16, name="middle_back")


def last_body(*refs):
    g1, parts, x, out = refs[0], refs[1:6], refs[6], refs[7]
    normed, inverse = stats(x[...].astype(F32))
    out[...] = g1[...] + norm_back(total_of(parts), normed, inverse)


def last(g1, parts, x, order=()):
    return kernel(last_body, shape((128, 2048), F32), (g1, *parts, x), order, name="last")


def mix_features(value):
    n = value.shape[0]
    return value.reshape(n, 2, 16, 64).transpose(0, 2, 1, 3).reshape(n, 2048)


def unmix_features(value):
    n = value.shape[0]
    return value.reshape(n, 16, 2, 64).transpose(0, 2, 1, 3).reshape(n, 2048)


def per_device(
    image_tokens,
    caption_embed,
    caption_lengths,
    output_grad,
    norm_self,
    norm_cross,
    norm_feed,
    self_query,
    self_key,
    self_value,
    self_output,
    cross_query,
    cross_key,
    cross_value,
    cross_output,
    up_weight,
    down_weight,
):
    xh = lax.axis_index("xh")
    xl = lax.axis_index("xl")
    core = lax.axis_index("c")
    place = [lax.axis_index("y"), lax.axis_index("z"), 2 * xh + xl, core]
    place = jnp.stack(place).astype(jnp.int32)
    gain_one = norm_self.astype(F32)[:, None]
    gain_two = norm_cross.astype(F32)[:, None]
    gain_three = norm_feed.astype(F32)[:, None]

    def gained(weight, gain):
        return (weight.astype(F32) * gain).astype(BF)

    def halves(weight):
        n = weight.shape[1] // 2
        first, second = weight[:, :n], weight[:, n:]
        return jnp.where(xh == 0, first, second), jnp.where(xh == 0, second, first)

    def in_order(mine, theirs):
        return jnp.where(xh == 0, mine, theirs), jnp.where(xh == 0, theirs, mine)

    def exchange(weights):
        pairs = [halves(w) for w in weights]
        mine = jnp.concatenate([p[0] for p in pairs], 1)
        theirs = swap(jnp.concatenate([p[1] for p in pairs], 1), "xh")
        return jnp.stack(in_order(mine, theirs), 0)

    def home(first, second):
        keep = jnp.where(xh == 0, first, second)
        theirs = swap(jnp.where(xh == 0, second, first).astype(BF), "xh")
        return keep, theirs.astype(F32)

    def join(keep, theirs):
        return jnp.concatenate(in_order(keep, theirs), 1)

    pair = exchange(
        (
            gained(self_query, gain_one),
            gained(self_key, gain_one),
            gained(self_value, gain_one),
            self_output.T,
            gained(cross_query, gain_two),
            cross_output.T,
        )
    )
    first = lax.all_gather(pair.reshape(128, 1536), PLANE, axis=0, tiled=True)
    resid = mix_features(image_tokens[0])
    normed_one, _ = stats(resid.astype(F32))
    grad_low = mix_features(output_grad[0])
    tokens = after(jnp.concatenate([normed_one.astype(BF), grad_low], 0), pair)
    pieces = [tokens, px(tokens, 1), px(tokens, -1)]
    caption = after(after(caption_embed[0], pieces[1]), pieces[2])
    caption = lax.all_gather(caption, ("xh", "xl", "c"), axis=0, tiled=True)
    caption = caption.reshape(64, 2, 16, 128).transpose(2, 0, 1, 3).reshape(16, 64, 256)
    pieces.append(jnp.concatenate(far_of(pieces[1], pieces[2]), 0))
    tokens = [side for piece in pieces for side in (piece, swap(piece, "c"))]
    pair_late = exchange(
        (
            after(gained(up_weight, gain_three), caption),
            down_weight.T,
            cross_key[:64],
            cross_value[:64],
            cross_key[64:],
            cross_value[64:],
        )
    )
    pair_kv = jnp.stack([pair_late[:, :, 2048:2560], pair_late[:, :, 2560:]], 1)
    pair_kv = pair_kv.reshape(256, 512)
    feed_weight = pair_late[:, :, :2048].reshape(128, 2048)
    feed_weight = lax.all_gather(feed_weight, PLANE, axis=0, tiled=True)
    caption = lax.all_to_all(caption, PLANE, split_axis=0, concat_axis=0, tiled=True)
    caption = caption.reshape(1024, 256)
    kv = dot(caption, pair_kv, 1, 0, BF).reshape(16, 64, 512)
    kv = lax.all_to_all(kv, PLANE, split_axis=0, concat_axis=0, tiled=True)
    qkv, p1, o1, keep, send = attend(0, 4, tokens, first)
    kv, both = fold(place, kv.reshape(16, 64, 512), first, [keep])
    kv_weight = lax.all_gather(after(pair_kv, kv), PLANE, axis=0, tiled=True)
    parts, low = reduce_tokens(keep, swap(send, "c"))
    both = hold(both, parts[2:4])
    slots_come = [px(both[1], -1), px(both[2], 1), px(both[3], 2)]
    slots = jnp.stack([both[0], *slots_come], 0)
    slots = (slots, swap(slots, "c"))

    length = jnp.where(xl == 0, caption_lengths[0, 0], caption_lengths[0, 1])[None]
    n2, i2, p2, x3, n3, i3 = middle(length, resid, parts, slots)

    theirs = swap(n3, "c")
    around = [px(n3, 1), px(n3, -1)]
    saved, keeps, others = None, [], []
    for i in range(4):
        if i == 0:
            mine = n3
        else:
            if i == 1:
                around = [hold(piece, keeps[:1]) for piece in around]
                across = far_of(*around)
            if i < 3:
                mine = around[i - 1]
            else:
                mine = jnp.concatenate([hold(piece, keeps[1:2]) for piece in across], 0)
            theirs = swap(mine, "c")
        *saved, keep, send = feed(
            i,
            mine,
            theirs,
            tokens[2 * i],
            tokens[2 * i + 1],
            feed_weight,
            saved and tuple(saved),
            others[:-1][-1:],
        )
        keeps.append(keep)
        others.append(swap(send, "c"))
    parts, low = reduce_tokens(keeps, others)
    act, grad, x3_all = saved
    total = feed_grad(x3_all, grad, act, tokens, low + [kv_weight])
    total = hold(total, parts[2:], True)
    g1, c1, keep_slots, send_slots = middle_back(
        grad_low, parts, slots, n2, i2, p2, n3, i3, [total]
    )
    total = lax.psum_scatter(total, PLANE, scatter_dimension=0, tiled=True)
    own, their_ff = home(total[:64], total[64:])
    own = own.astype(F32)
    up_out = join(own[:, :1024], their_ff[:, :1024])
    down_out = join(own[:, 1024:], their_ff[:, 1024:])

    theirs = swap(c1, "c")
    around = [px(c1, 1), px(c1, -1)]
    slot_back = keep_slots.astype(F32) + swap(send_slots, "c").astype(F32)
    back, keeps, others = None, [], []
    for i in range(4):
        if i == 0:
            mine = c1
        else:
            if i == 1:
                around = [hold(piece, keeps[:1]) for piece in around]
                across = far_of(*around)
                slot_back = after(slot_back.astype(BF), around[1])
                slot_back = [
                    slot_back[0],
                    px(slot_back[1], 1),
                    px(slot_back[2], -1),
                    px(slot_back[3], 2),
                ]
            if i < 3:
                mine = around[i - 1]
            else:
                mine = jnp.concatenate([hold(piece, keeps[1:2]) for piece in across], 0)
            theirs = swap(mine, "c")
        order = others[:-1][-1:] + (slot_back[1:] if i == 3 else [])
        *back, keep, send = attend_back(
            i, mine, theirs, first, qkv, p1, back and tuple(back), order
        )
        keeps.append(keep)
        others.append(swap(send, "c"))
    parts, low = reduce_tokens(keeps, others)
    cross_grad, grad_kv = unfold(place, slot_back, kv, first)
    more = more_grad(*back, o1, cross_grad, tokens, keeps[-1:])
    kv_all = lax.all_to_all(
        jnp.broadcast_to(grad_kv[None], (16, 64, 512)),
        PLANE,
        split_axis=0,
        concat_axis=0,
        tiled=True,
    ).reshape(1024, 512)
    kv_grad = dot(caption, kv_all, 0, 0)
    ck_own, ck_their = home(kv_grad[:128], kv_grad[128:])
    ck_out = join(ck_own[:, :256], ck_their[:, :256])
    cv_out = join(ck_own[:, 256:], ck_their[:, 256:])
    more = hold(more, [total, ck_their, low[-1]], True)
    y_keep, y_send = feed_out(act, feed_weight, [more])
    rest = lax.psum_scatter(more, PLANE, scatter_dimension=0, tiled=True)
    y_parts, _ = reduce_tokens(y_keep, swap(y_send, "c"))
    block_out = x3
    for part in y_parts:
        block_out = block_out + part.astype(F32)
    grad_kv = after(grad_kv, more)
    cap_grad = dot(grad_kv, kv_weight, 1, 1, BF).reshape(4, 16, 4096)
    keep = jnp.where(core == 0, cap_grad[:, :8], cap_grad[:, 8:])
    send = jnp.where(core == 0, cap_grad[:, 8:], cap_grad[:, :8])
    send = swap(send, "c")
    low_cap = (keep.astype(F32) + send.astype(F32)).astype(BF)
    near_image = [pick(low_cap, place[2] + n) for n in range(4)]
    cap_out = near_image[0].astype(F32)
    for n in (1, 2, 3):
        cap_out = cap_out + px(near_image[n], n).astype(F32)
    cap_out = cap_out.reshape(8, 16, 2, 128).transpose(0, 2, 1, 3).reshape(1, 8, 4096)
    rest = hold(rest, y_parts[2:], True)
    own, their = home(rest[:64], rest[64:])
    own = own.astype(F32)
    outs = [join(own[:, at : at + 256], their[:, at : at + 256]) for at in range(0, 1536, 256)]
    so_out, cq_out, co_out = outs[3:]

    image_grad = unmix_features(last(g1, parts, resid))[None]

    first_gain = (
        jnp.sum(outs[0] * self_query.astype(F32), 1)
        + jnp.sum(outs[1] * self_key.astype(F32), 1)
        + jnp.sum(outs[2] * self_value.astype(F32), 1)
    )
    terms = jnp.stack(
        [
            first_gain,
            jnp.sum(cq_out * cross_query.astype(F32), 1),
            jnp.sum(up_out * up_weight.astype(F32), 1),
        ],
        0,
    )
    terms = terms + swap(terms, "xl")
    terms = terms + swap(terms, "c")

    return (
        unmix_features(block_out.astype(BF))[None],
        image_grad,
        cap_out,
        terms[0],
        terms[1],
        terms[2],
        outs[0] * gain_one,
        outs[1] * gain_one,
        outs[2] * gain_one,
        so_out.T,
        cq_out * gain_two,
        ck_out,
        cv_out,
        co_out.T,
        up_out * gain_three,
        down_out.T,
    )


def solution(mesh):
    names = ("xh", "y", "z", "xl", "c")
    fine = Mesh(mesh.devices.reshape(2, 4, 4, 2, 2), names)
    rows, text = ("xh", "y", "z"), ("xl", "c")
    tokens = P(rows, text, None)
    by_row = P(rows, text)
    by_text = P(text, rows)
    weights = (by_row, by_row, by_row, by_text, by_row, by_row, by_row, by_text, by_row, by_text)
    in_specs = (tokens, tokens, P(rows, None), tokens) + (P(rows),) * 3 + weights
    out_specs = (tokens,) * 3 + (P(rows),) * 3 + weights
    return jax.shard_map(
        per_device, mesh=fine, in_specs=in_specs, out_specs=out_specs, check_vma=False
    )
```

profile of v0, /device:TPU:1, one launch (start us, length us, event | category | flops | bytes accessed | tf_op | source)
XLA Modules:
  0.0 504.4 jit_solution(14865012336248607062)
XLA Ops:
  15.9 4.2 collective-permute-done
  27.4 21.7 %collective-permute-done.2.refs_2_.ga.refs_5_.refs_6_ = bf16[256,2048]{1,0:T(8,128)(2,1)S(1)} collective-permute-done((bf16[256,2048]{1,0:T(8,128)(2,1)S(1)}, bf16[256,2048]{1,0:T(8,128)(2,1)S(1)}, u32[]{:S(2)}, u32[]{:S(2)}) %collective-permute-start.2) | collective-permute-done | bytes 1048608 | tf_op jit(solution)/shard_map/ppermute | solution.py:91
  51.6 15.3 %all-gather = bf16[1,64,4096]{2,1,0:T(8,128)(2,1)S(1)} all-gather(bf16[1,8,4096]{2,1,0:T(8,128)(2,1)S(1)} %add_convert_fusion.18), channel_id=2, replica_groups=mesh['xh'=2,'y'=4,'z'=4,'xl'=2,'c'=2] {'xh','xl','c'}, dimensions={1}, use_global_device_ids=true | all-gather | bytes 589824 | tf_op jit(solution)/shard_map/all_gather | solution.py:557
  76.5 10.8 %collective-permute-done.13 = bf16[64,3072]{1,0:T(8,128)(2,1)S(1)} collective-permute-done((bf16[64,3072]{1,0:T(8,128)(2,1)S(1)}, bf16[64,3072]{1,0:T(8,128)(2,1)S(1)}, u32[]{:S(2)}, u32[]{:S(2)}) %collective-permute-start.13) | collective-permute-done | bytes 393248 | tf_op jit(solution)/shard_map/ppermute | solution.py:99
  94.1 8.7 %collective-permute-done.6 = bf16[128,2048]{1,0:T(8,128)(2,1)S(1)} collective-permute-done((bf16[128,2048]{1,0:T(8,128)(2,1)S(1)}, bf16[128,2048]{1,0:T(8,128)(2,1)S(1)}, u32[]{:S(2)}, u32[]{:S(2)}) %collective-permute-start.6) | collective-permute-done | bytes 524320 | tf_op jit(solution)/shard_map/ppermute | solution.py:91
  106.4 8.1 %all-to-all-start = ((bf16[16,64,256]{2,1,0:T(8,128)(2,1)}), bf16[16,64,256]{2,1,0:T(8,128)(2,1)}, u32[]{:S(2)}, u32[]{:S(2)}) async-start(bf16[16,64,256]{2,1,0:T(8,128)(2,1)} %reshape.171), calls=%async_computation | async-start | bytes 1048576 | tf_op jit(solution)/shard_map/all_to_all | solution.py:575
  115.5 9.2 %all-to-all-done = bf16[16,64,256]{2,1,0:T(8,128)(2,1)} async-done(((bf16[16,64,256]{2,1,0:T(8,128)(2,1)}), bf16[16,64,256]{2,1,0:T(8,128)(2,1)}, u32[]{:S(2)}, u32[]{:S(2)}) %all-to-all-start) | async-done | bytes 524320 | tf_op jit(solution)/shard_map/all_to_all | solution.py:575
  127.2 4.4 all-to-all-start.1
  134.9 12.1 %attend.1 = (bf16[1024,768]{1,0:T(8,128)(2,1)S(1)}, bf16[4,2,256,256]{3,2,1,0:T(8,128)(2,1)S(1)}, bf16[1024,256]{1,0:T(8,128)(2,1)S(1)}, bf16[4,128,2048]{2,1,0:T(8,128)(2,1)S(1)}, bf16[4,128,2048]{2,1,0:T(8,128)(2,1)}) custom-call(bf16[256,2048]{1,0:T(8,128)(2,1)S(1)} %add_convert_fusion.2.refs_0_.ga.refs_3_.refs_4_, ...), custom_call_target="tpu_custom_call" | custom-call | flops 1000 | bytes 1000 | tf_op jit(solution)/shard_map/attend/pallas_call | solution.py:58
  166.5 7.5 %collective-permute-done.10.refs_1_.refs_3_ = bf16[128,2048]{1,0:T(8,128)(2,1)S(1)} collective-permute-done((bf16[128,2048]{1,0:T(8,128)(2,1)S(1)}, bf16[128,2048]{1,0:T(8,128)(2,1)S(1)}, u32[]{:S(2)}, u32[]{:S(2)}) %collective-permute-start.10) | collective-permute-done | bytes 524320 | tf_op jit(solution)/shard_map/ppermute | solution.py:91
  184.1 5.0 collective-permute-done.15
  191.2 5.8 %collective-permute-start.17 = (bf16[4,64,2048]{2,1,0:T(8,128)(2,1)S(1)}, bf16[4,64,2048]{2,1,0:T(8,128)(2,1)}, u32[]{:S(2)}, u32[]{:S(2)}) collective-permute-start(bf16[4,64,2048]{2,1,0:T(8,128)(2,1)S(1)} %pad_maximum_fusion.refs_6_), channel_id=1, source_target_pairs={{0,1},{1,0},{2,3},{3,2},{4,5},{5,4},{6,7},{7,6},{8,9},{9,8},{10,11... | collective-permute-start | bytes 3145736 | tf_op jit(solution)/shard_map/ppermute | solution.py:99
  202.9 11.6 %collective-permute-done.12.refs_5_ = bf16[128,2048]{1,0:T(8,128)(2,1)S(1)} collective-permute-done((bf16[128,2048]{1,0:T(8,128)(2,1)}, bf16[128,2048]{1,0:T(8,128)(2,1)S(1)}, u32[]{:S(2)}, u32[]{:S(2)}) %collective-permute-start.12) | collective-permute-done | bytes 524320 | tf_op jit(solution)/shard_map/ppermute | solution.py:91
  216.6 4.0 middle.1
  231.3 5.3 %feed.4 = (bf16[1024,1024]{1,0:T(8,128)(2,1)S(1)}, bf16[1024,1024]{1,0:T(8,128)(2,1)S(1)}, bf16[1024,2048]{1,0:T(8,128)(2,1)S(1)}, bf16[128,2048]{1,0:T(8,128)(2,1)S(1)}, bf16[128,2048]{1,0:T(8,128)(2,1)S(1)}) custom-call(bf16[128,2048]{1,0:T(8,128)(2,1)} %get-tuple-element.77.xa.refs_11_, bf16[128,2048]{1,0:T(8,128)(2,1)S(1)} %copy-done.73, ...), custom_call_target="tpu_custom_call" | custom-call | flops 1000 | bytes 1000 | tf_op jit(solution)/shard_map/feed/pallas_call | solution.py:58
  244.5 5.1 %feed.5 = (bf16[1024,1024]{1,0:T(8,128)(2,1)S(1)}, bf16[1024,1024]{1,0:T(8,128)(2,1)S(1)}, bf16[1024,2048]{1,0:T(8,128)(2,1)S(1)}, bf16[128,2048]{1,0:T(8,128)(2,1)S(1)}, bf16[128,2048]{1,0:T(8,128)(2,1)S(1)}) custom-call(bf16[128,2048]{1,0:T(8,128)(2,1)} %hold.13.xa, ...), custom_call_target="tpu_custom_call", output_to_operand_aliasing={{0}: (5, {}), {1}: (6, {}), {2}: (7, {})} | custom-call | flops 1000 | bytes 1000 | tf_op jit(solution)/shard_map/feed/pallas_call | solution.py:58
  251.5 5.3 %feed.6 = (bf16[1024,1024]{1,0:T(8,128)(2,1)S(1)}, bf16[1024,1024]{1,0:T(8,128)(2,1)S(1)}, bf16[1024,2048]{1,0:T(8,128)(2,1)S(1)}, bf16[128,2048]{1,0:T(8,128)(2,1)S(1)}, bf16[128,2048]{1,0:T(8,128)(2,1)S(1)}) custom-call(bf16[128,2048]{1,0:T(8,128)(2,1)} %hold.15.refs_0_, ...), custom_call_target="tpu_custom_call", output_to_operand_aliasing={{0}: (5, {}), {1}: (6, {}), {2}: (7, {})} | custom-call | flops 1000 | bytes 1000 | tf_op jit(solution)/shard_map/feed/pallas_call | solution.py:58
  257.3 5.3 %feed.7 = (bf16[1024,1024]{1,0:T(8,128)(2,1)S(1)}, bf16[1024,1024]{1,0:T(8,128)(2,1)S(1)}, bf16[1024,2048]{1,0:T(8,128)(2,1)S(1)}, bf16[128,2048]{1,0:T(8,128)(2,1)S(1)}, bf16[128,2048]{1,0:T(8,128)(2,1)S(1)}) custom-call(bf16[128,2048]{1,0:T(8,128)(2,1)S(1)} %pad_maximum_fusion.2.refs_0_, ...), custom_call_target="tpu_custom_call", output_to_operand_aliasing={{0}: (5, {}), {1}: (6, {}), {2}: (7, {})} | custom-call | flops 1000 | bytes 1000 | tf_op jit(solution)/shard_map/feed/pallas_call | solution.py:58
  273.7 12.9 %feed_grad.1.refs_0_ = bf16[2048,2048]{1,0:T(8,128)(2,1)} custom-call(bf16[1024,2048]{1,0:T(8,128)(2,1)S(1)} %copy-done.5, bf16[1024,1024]{1,0:T(8,128)(2,1)S(1)} %copy-done.10, bf16[1024,1024]{1,0:T(8,128)(2,1)S(1)} %get-tuple-element.91.refs_2_.refs_0_, bf16[256,2048]{1,0:T(8,128)(2,1)} %copy-done.11, ...), custom_call_target="tpu_custom_call" | custom-call | flops 1000 | bytes 1000 | tf_op jit(solution)/shard_map/feed_grad/pallas_call | solution.py:58
  295.7 4.6 middle_back.1
  307.5 7.6 %collective-permute-done.37.refs_0_ = bf16[128,2048]{1,0:T(8,128)(2,1)S(1)} collective-permute-done((bf16[128,2048]{1,0:T(8,128)(2,1)S(1)}, bf16[128,2048]{1,0:T(8,128)(2,1)S(1)}, u32[]{:S(2)}, u32[]{:S(2)}) %collective-permute-start.37) | collective-permute-done | bytes 524320 | tf_op jit(solution)/shard_map/ppermute | solution.py:91
  326.8 9.1 %collective-permute-done.44.refs_8_.b1 = bf16[64,2048]{1,0:T(8,128)(2,1)S(1)} collective-permute-done((bf16[64,2048]{1,0:T(8,128)(2,1)S(1)}, bf16[64,2048]{1,0:T(8,128)(2,1)S(1)}, u32[]{:S(2)}, u32[]{:S(2)}) %collective-permute-start.44) | collective-permute-done | bytes 262176 | tf_op jit(solution)/shard_map/ppermute | solution.py:91
  341.3 7.7 %all-to-all-start.2 = ((bf16[16,64,512]{2,1,0:T(8,128)(2,1)}), bf16[16,64,512]{2,1,0:T(8,128)(2,1)}, u32[]{:S(2)}, u32[]{:S(2)}) async-start(bf16[16,64,512]{2,1,0:T(8,128)(2,1)} %broadcast_in_dim.5), calls=%async_computation.3 | async-start | bytes 2097152 | tf_op jit(solution)/shard_map/all_to_all | solution.py:663
  372.3 9.9 %more_grad.1.refs_0_ = bf16[2048,1536]{1,0:T(8,128)(2,1)} custom-call(bf16[1024,768]{1,0:T(8,128)(2,1)S(1)} %get-tuple-element.118.refs_0_, bf16[1024,2048]{1,0:T(8,128)(2,1)S(1)} %get-tuple-element.119.refs_1_, bf16[1024,256]{1,0:T(8,128)(2,1)S(1)} %copy-done.67, bf16[2048,512]{1,0:T(8,128)(2,1)S(1)} %copy-done.43, bf16[256,2048]{1,0:T(8,128)(2,1)} %copy-done.11, ...), custom_call_target="tpu_custom_call" | custom-call | flops 1000 | bytes 1000 | tf_op jit(solution)/shard_map/more_grad/pallas_call | solution.py:58
  385.3 6.2 %collective-permute-done.47 = bf16[128,512]{1,0:T(8,128)(2,1)S(1)} collective-permute-done((bf16[128,512]{1,0:T(8,128)(2,1)S(1)}, bf16[128,512]{1,0:T(8,128)(2,1)S(1)}, u32[]{:S(2)}, u32[]{:S(2)}) %collective-permute-start.47) | collective-permute-done | bytes 131104 | tf_op jit(solution)/shard_map/ppermute | solution.py:99
  402.4 9.5 %collective-permute-done.55.refs_4_ = bf16[128,2048]{1,0:T(8,128)(2,1)S(1)} collective-permute-done((bf16[128,2048]{1,0:T(8,128)(2,1)S(1)}, bf16[128,2048]{1,0:T(8,128)(2,1)S(1)}, u32[]{:S(2)}, u32[]{:S(2)}) %collective-permute-start.55) | collective-permute-done | bytes 524320 | tf_op jit(solution)/shard_map/ppermute | solution.py:91
  412.5 11.3 %collective-permute-done.56.refs_5_ = bf16[128,2048]{1,0:T(8,128)(2,1)S(1)} collective-permute-done((bf16[128,2048]{1,0:T(8,128)(2,1)S(1)}, bf16[128,2048]{1,0:T(8,128)(2,1)S(1)}, u32[]{:S(2)}, u32[]{:S(2)}) %collective-permute-start.56) | collective-permute-done | bytes 524320 | tf_op jit(solution)/shard_map/ppermute | solution.py:91
  426.6 10.3 %feed_out.1 = (bf16[4,128,2048]{2,1,0:T(8,128)(2,1)}, bf16[4,128,2048]{2,1,0:T(8,128)(2,1)}) custom-call(bf16[1024,1024]{1,0:T(8,128)(2,1)} %copy-done.8, bf16[2048,2048]{1,0:T(8,128)(2,1)} %all-gather.7.cloned.1.call-done.w_ref.refs_4_.refs_1_, bf16[2048,1536]{1,0:T(8,128)(2,1)} %hold.22.refs_2_), custom_call_target="tpu_custom_call" | custom-call | flops 1000 | bytes 1000 | tf_op jit(solution)/shard_map/feed_out/pallas_call | solution.py:58
  457.5 7.1 %collective-permute-done.50.refs_1_ = bf16[128,2048]{1,0:T(8,128)(2,1)S(1)} collective-permute-done((bf16[128,2048]{1,0:T(8,128)(2,1)S(1)}, bf16[128,2048]{1,0:T(8,128)(2,1)S(1)}, u32[]{:S(2)}, u32[]{:S(2)}) %collective-permute-start.50) | collective-permute-done | bytes 524320 | tf_op jit(solution)/shard_map/ppermute | solution.py:91
  464.6 4.0 collective-permute-start.60
  468.6 8.1 %collective-permute-done.52.refs_3_ = bf16[128,2048]{1,0:T(8,128)(2,1)S(1)} collective-permute-done((bf16[128,2048]{1,0:T(8,128)(2,1)S(1)}, bf16[128,2048]{1,0:T(8,128)(2,1)S(1)}, u32[]{:S(2)}, u32[]{:S(2)}) %collective-permute-start.52) | collective-permute-done | bytes 524320 | tf_op jit(solution)/shard_map/ppermute | solution.py:91
  489.1 7.2 %collective-permute-start.64 = (f32[3,64]{1,0:T(4,128)S(1)}, f32[3,64]{1,0:T(4,128)S(1)}, u32[]{:S(2)}, u32[]{:S(2)}) collective-permute-start(f32[3,64]{1,0:T(4,128)S(1)} %fusion.30), channel_id=1, source_target_pairs={{0,1},{1,0},{2,3},{3,2},{4,5},{5,4},{6,7},{7,6},{8,9},{9,8},{10,11... | collective-permute-start | bytes 2312 | tf_op jit(solution)/shard_map/ppermute | solution.py:99
  (466 shorter events, 217.8 us)
Async XLA Ops:
  7.2 124.8 %all-gather.5.cloned.1.call-start = ((), (), s32[]{:S(2)}) async-start(), calls=%async_computation.5 | async-start | bytes 6684672 | tf_op jit(solution)/shard_map/all_gather | solution.py:550
  20.9 205.9 %all-gather.7.cloned.1.call-start = ((), (), s32[]{:S(2)}) async-start(), calls=%async_computation.6 | async-start | bytes 8912896 | tf_op jit(solution)/shard_map/all_gather | solution.py:574
  24.4 24.7 %collective-permute-start.2 = (bf16[256,2048]{1,0:T(8,128)(2,1)S(1)}, bf16[256,2048]{1,0:T(8,128)(2,1)S(1)}, u32[]{:S(2)}, u32[]{:S(2)}) collective-permute-start(bf16[256,2048]{1,0:T(8,128)(2,1)S(1)} %add_convert_fusion.2.refs_0_.ga.refs_3_.refs_4_), channel_id=1, source_target_pairs={{0,2},{2,64},{64,66},{66,0},{1,3},{3,65},{65,67},{67,1},{4,6},{6,6... | collective-permute-start | bytes 3145736 | tf_op jit(solution)/shard_map/ppermute | solution.py:91
  26.1 24.2 %collective-permute-start.4 = (bf16[256,2048]{1,0:T(8,128)(2,1)S(1)}, bf16[256,2048]{1,0:T(8,128)(2,1)S(1)}, u32[]{:S(2)}, u32[]{:S(2)}) collective-permute-start(bf16[256,2048]{1,0:T(8,128)(2,1)S(1)} %add_convert_fusion.2.refs_0_.ga.refs_3_.refs_4_), channel_id=1, source_target_pairs={{0,66},{2,0},{64,2},{66,64},{1,67},{3,1},{65,3},{67,65},{4,70},{6,... | collective-permute-start | bytes 3145736 | tf_op jit(solution)/shard_map/ppermute | solution.py:91
  92.0 40.0 %collective-permute-start.1 = (bf16[256,2048]{1,0:T(8,128)(2,1)S(1)}, bf16[256,2048]{1,0:T(8,128)(2,1)}, u32[]{:S(2)}, u32[]{:S(2)}) collective-permute-start(bf16[256,2048]{1,0:T(8,128)(2,1)S(1)} %add_convert_fusion.2.refs_0_.ga.refs_3_.refs_4_), channel_id=1, source_target_pairs={{0,1},{1,0},{2,3},{3,2},{4,5},{5,4},{6,7},{7,6},{8,9},{9,8},{10,11... | collective-permute-start | bytes 3145736 | tf_op jit(solution)/shard_map/ppermute | solution.py:99
  93.5 38.4 %collective-permute-start.3 = (bf16[256,2048]{1,0:T(8,128)(2,1)S(1)}, bf16[256,2048]{1,0:T(8,128)(2,1)}, u32[]{:S(2)}, u32[]{:S(2)}) collective-permute-start(bf16[256,2048]{1,0:T(8,128)(2,1)S(1)} %collective-permute-done.2.refs_2_.ga.refs_5_.refs_6_), channel_id=1, source_target_pairs={{0,1},{1,0},{2,3},{3,2},{4,5},{5,4},{6,7},{7,6},{8,9},{9,8},{10,11... | collective-permute-start | bytes 3145736 | tf_op jit(solution)/shard_map/ppermute | solution.py:99
  93.6 38.4 %collective-permute-start.5 = (bf16[256,2048]{1,0:T(8,128)(2,1)S(1)}, bf16[256,2048]{1,0:T(8,128)(2,1)}, u32[]{:S(2)}, u32[]{:S(2)}) collective-permute-start(bf16[256,2048]{1,0:T(8,128)(2,1)S(1)} %collective-permute-done.4.refs_4_.refs_2_.refs_7_.refs_8_), channel_id=1, source_target_pairs={{0,1},{1,0},{2,3},{3,2},{4,5},{5,4},{6,7},{7,6},{8,9},{9,8},{10,11... | collective-permute-start | bytes 3145736 | tf_op jit(solution)/shard_map/ppermute | solution.py:99
  104.5 27.5 %collective-permute-start.8 = (bf16[256,2048]{1,0:T(8,128)(2,1)}, bf16[256,2048]{1,0:T(8,128)(2,1)}, u32[]{:S(2)}, u32[]{:S(2)}) collective-permute-start(bf16[256,2048]{1,0:T(8,128)(2,1)} %constant_dynamic-update-slice_fusion.12.refs_6_.refs_2_.refs_9_.refs_10_), channel_id=1, source_target_pairs={{0,1},{1,0},{2,3},{3,2},{4,5},{5,4},{6,7},{7,6},{8,9},{9,8},{10,11... | collective-permute-start | bytes 3145736 | tf_op jit(solution)/shard_map/ppermute | solution.py:99
  106.4 18.3 %all-to-all-start = ((bf16[16,64,256]{2,1,0:T(8,128)(2,1)}), bf16[16,64,256]{2,1,0:T(8,128)(2,1)}, u32[]{:S(2)}, u32[]{:S(2)}) async-start(bf16[16,64,256]{2,1,0:T(8,128)(2,1)} %reshape.171), calls=%async_computation | async-start | bytes 1048576 | tf_op jit(solution)/shard_map/all_to_all | solution.py:575
  127.2 28.4 %all-to-all-start.1 = ((bf16[16,64,512]{2,1,0:T(8,128)(2,1)}), bf16[16,64,512]{2,1,0:T(8,128)(2,1)}, u32[]{:S(2)}, u32[]{:S(2)}) async-start(bf16[16,64,512]{2,1,0:T(8,128)(2,1)} %bitcast.145), calls=%async_computation.1 | async-start | bytes 2097152 | tf_op jit(solution)/shard_map/all_to_all | solution.py:578
  131.6 138.3 %all-gather.9.cloned.1.call-start = ((), (), s32[]{:S(2)}) async-start(), calls=%async_computation.7 | async-start | bytes 4456448 | tf_op jit(solution)/shard_map/all_gather | solution.py:581
  161.5 230.1 %reduce-scatter.3.cloned.1.call-start = ((), (), s32[]{:S(2)}) async-start(), calls=%async_computation.8 | async-start | bytes 8912896 | tf_op jit(solution)/shard_map/reduce_scatter | solution.py:625
  191.2 23.3 %collective-permute-start.17 = (bf16[4,64,2048]{2,1,0:T(8,128)(2,1)S(1)}, bf16[4,64,2048]{2,1,0:T(8,128)(2,1)}, u32[]{:S(2)}, u32[]{:S(2)}) collective-permute-start(bf16[4,64,2048]{2,1,0:T(8,128)(2,1)S(1)} %pad_maximum_fusion.refs_6_), channel_id=1, source_target_pairs={{0,1},{1,0},{2,3},{3,2},{4,5},{5,4},{6,7},{7,6},{8,9},{9,8},{10,11... | collective-permute-start | bytes 3145736 | tf_op jit(solution)/shard_map/ppermute | solution.py:99
  198.8 15.7 %collective-permute-start.12 = (bf16[128,2048]{1,0:T(8,128)(2,1)}, bf16[128,2048]{1,0:T(8,128)(2,1)S(1)}, u32[]{:S(2)}, u32[]{:S(2)}) collective-permute-start(bf16[128,2048]{1,0:T(8,128)(2,1)} %get-tuple-element.149), channel_id=1, source_target_pairs={{0,64},{2,66},{64,0},{66,2},{1,65},{3,67},{65,1},{67,3},{4,68},{6,... | collective-permute-start | bytes 1572872 | tf_op jit(solution)/shard_map/ppermute | solution.py:91
  223.4 15.1 %collective-permute-start.18 = (bf16[128,2048]{1,0:T(8,128)(2,1)}, bf16[128,2048]{1,0:T(8,128)(2,1)}, u32[]{:S(2)}, u32[]{:S(2)}) collective-permute-start(bf16[128,2048]{1,0:T(8,128)(2,1)} %get-tuple-element.77.xa.refs_11_), channel_id=1, source_target_pairs={{0,2},{2,64},{64,66},{66,0},{1,3},{3,65},{65,67},{67,1},{4,6},{6,6... | collective-permute-start | bytes 1572872 | tf_op jit(solution)/shard_map/ppermute | solution.py:91
  223.4 15.9 %collective-permute-start.22 = (bf16[128,2048]{1,0:T(8,128)(2,1)}, bf16[128,2048]{1,0:T(8,128)(2,1)}, u32[]{:S(2)}, u32[]{:S(2)}) collective-permute-start(bf16[128,2048]{1,0:T(8,128)(2,1)} %get-tuple-element.77.xa.refs_11_), channel_id=1, source_target_pairs={{0,66},{2,0},{64,2},{66,64},{1,67},{3,1},{65,3},{67,65},{4,70},{6,... | collective-permute-start | bytes 1572872 | tf_op jit(solution)/shard_map/ppermute | solution.py:91
  264.1 23.8 %collective-permute-start.30 = (bf16[128,2048]{1,0:T(8,128)(2,1)S(1)}, bf16[128,2048]{1,0:T(8,128)(2,1)}, u32[]{:S(2)}, u32[]{:S(2)}) collective-permute-start(bf16[128,2048]{1,0:T(8,128)(2,1)S(1)} %add_convert_fusion.10.refs_12_), channel_id=1, source_target_pairs={{0,2},{2,64},{64,66},{66,0},{1,3},{3,65},{65,67},{67,1},{4,6},{6,6... | collective-permute-start | bytes 1572872 | tf_op jit(solution)/shard_map/ppermute | solution.py:91
  265.4 22.6 %collective-permute-start.28 = (bf16[128,2048]{1,0:T(8,128)(2,1)S(1)}, bf16[128,2048]{1,0:T(8,128)(2,1)}, u32[]{:S(2)}, u32[]{:S(2)}) collective-permute-start(bf16[128,2048]{1,0:T(8,128)(2,1)S(1)} %add_convert_fusion.11.refs_11_), channel_id=1, source_target_pairs={{0,66},{2,0},{64,2},{66,64},{1,67},{3,1},{65,3},{67,65},{4,70},{6,... | collective-permute-start | bytes 1572872 | tf_op jit(solution)/shard_map/ppermute | solution.py:91
  268.7 23.0 %collective-permute-start.32 = (bf16[128,2048]{1,0:T(8,128)(2,1)}, bf16[128,2048]{1,0:T(8,128)(2,1)}, u32[]{:S(2)}, u32[]{:S(2)}) collective-permute-start(bf16[128,2048]{1,0:T(8,128)(2,1)} %add_convert_fusion.9.refs_13_), channel_id=1, source_target_pairs={{0,64},{2,66},{64,0},{66,2},{1,65},{3,67},{65,1},{67,3},{4,68},{6,... | collective-permute-start | bytes 1572872 | tf_op jit(solution)/shard_map/ppermute | solution.py:91
  300.3 20.2 %collective-permute-start.43 = (bf16[4,64,2048]{2,1,0:T(8,128)(2,1)S(1)}, bf16[4,64,2048]{2,1,0:T(8,128)(2,1)S(1)}, u32[]{:S(2)}, u32[]{:S(2)}) collective-permute-start(bf16[4,64,2048]{2,1,0:T(8,128)(2,1)S(1)} %get-tuple-element.117), channel_id=1, source_target_pairs={{0,1},{1,0},{2,3},{3,2},{4,5},{5,4},{6,7},{7,6},{8,9},{9,8},{10,11... | collective-permute-start | bytes 3145736 | tf_op jit(solution)/shard_map/ppermute | solution.py:99
  318.9 31.9 %collective-permute-start.36 = (bf16[128,2048]{1,0:T(8,128)(2,1)}, bf16[128,2048]{1,0:T(8,128)(2,1)}, u32[]{:S(2)}, u32[]{:S(2)}) collective-permute-start(bf16[128,2048]{1,0:T(8,128)(2,1)} %hold.18.ca), channel_id=1, source_target_pairs={{0,1},{1,0},{2,3},{3,2},{4,5},{5,4},{6,7},{7,6},{8,9},{9,8},{10,11... | collective-permute-start | bytes 1572872 | tf_op jit(solution)/shard_map/ppermute | solution.py:99
  321.0 14.8 %collective-permute-start.44 = (bf16[64,2048]{1,0:T(8,128)(2,1)S(1)}, bf16[64,2048]{1,0:T(8,128)(2,1)S(1)}, u32[]{:S(2)}, u32[]{:S(2)}) collective-permute-start(bf16[64,2048]{1,0:T(8,128)(2,1)S(1)} %get-tuple-element.159), channel_id=1, source_target_pairs={{0,2},{2,64},{64,66},{66,0},{1,3},{3,65},{65,67},{67,1},{4,6},{6,6... | collective-permute-start | bytes 786440 | tf_op jit(solution)/shard_map/ppermute | solution.py:91
  325.5 37.0 %collective-permute-start.35 = (bf16[64,2048]{1,0:T(8,128)(2,1)}, bf16[64,2048]{1,0:T(8,128)(2,1)}, u32[]{:S(2)}, u32[]{:S(2)}) collective-permute-start(bf16[64,2048]{1,0:T(8,128)(2,1)} %slice.434), channel_id=1, source_target_pairs={{0,2},{2,64},{64,66},{66,0},{1,3},{3,65},{65,67},{67,1},{4,6},{6,6... | collective-permute-start | bytes 786440 | tf_op jit(solution)/shard_map/ppermute | solution.py:91
  335.8 26.7 %collective-permute-start.38 = (bf16[64,2048]{1,0:T(8,128)(2,1)}, bf16[64,2048]{1,0:T(8,128)(2,1)}, u32[]{:S(2)}, u32[]{:S(2)}) collective-permute-start(bf16[64,2048]{1,0:T(8,128)(2,1)} %slice.435), channel_id=1, source_target_pairs={{0,66},{2,0},{64,2},{66,64},{1,67},{3,1},{65,3},{67,65},{4,70},{6,... | collective-permute-start | bytes 786440 | tf_op jit(solution)/shard_map/ppermute | solution.py:91
  341.3 41.6 %all-to-all-start.2 = ((bf16[16,64,512]{2,1,0:T(8,128)(2,1)}), bf16[16,64,512]{2,1,0:T(8,128)(2,1)}, u32[]{:S(2)}, u32[]{:S(2)}) async-start(bf16[16,64,512]{2,1,0:T(8,128)(2,1)} %broadcast_in_dim.5), calls=%async_computation.3 | async-start | bytes 2097152 | tf_op jit(solution)/shard_map/all_to_all | solution.py:663
  349.1 127.6 %reduce-scatter.5.cloned.1.call-start = ((), (), s32[]{:S(2)}) async-start(), calls=%async_computation.9 | async-start | bytes 6684672 | tf_op jit(solution)/shard_map/reduce_scatter | solution.py:676
  349.1 15.8 %collective-permute-start.40 = (bf16[128,2048]{1,0:T(8,128)(2,1)}, bf16[128,2048]{1,0:T(8,128)(2,1)S(1)}, u32[]{:S(2)}, u32[]{:S(2)}) collective-permute-start(bf16[128,2048]{1,0:T(8,128)(2,1)} %copy-done.40), channel_id=1, source_target_pairs={{0,1},{1,0},{2,3},{3,2},{4,5},{5,4},{6,7},{7,6},{8,9},{9,8},{10,11... | collective-permute-start | bytes 1572872 | tf_op jit(solution)/shard_map/ppermute | solution.py:99
  400.4 23.4 %collective-permute-start.56 = (bf16[128,2048]{1,0:T(8,128)(2,1)S(1)}, bf16[128,2048]{1,0:T(8,128)(2,1)S(1)}, u32[]{:S(2)}, u32[]{:S(2)}) collective-permute-start(bf16[128,2048]{1,0:T(8,128)(2,1)S(1)} %add_convert_fusion.8.refs_3_), channel_id=1, source_target_pairs={{0,64},{2,66},{64,0},{66,2},{1,65},{3,67},{65,1},{67,3},{4,68},{6,... | collective-permute-start | bytes 1572872 | tf_op jit(solution)/shard_map/ppermute | solution.py:91
  443.5 36.2 %collective-permute-start.58 = (bf16[8,4096]{1,0:T(8,128)(2,1)S(1)}, bf16[8,4096]{1,0:T(8,128)(2,1)S(1)}, u32[]{:S(2)}, u32[]{:S(2)}) collective-permute-start(bf16[8,4096]{1,0:T(8,128)(2,1)S(1)} %get-tuple-element.192), channel_id=1, source_target_pairs={{0,2},{2,64},{64,66},{66,0},{1,3},{3,65},{65,67},{67,1},{4,6},{6,6... | collective-permute-start | bytes 196616 | tf_op jit(solution)/shard_map/ppermute | solution.py:91
  444.9 34.8 %collective-permute-start.59 = (bf16[8,4096]{1,0:T(8,128)(2,1)S(1)}, bf16[8,4096]{1,0:T(8,128)(2,1)S(1)}, u32[]{:S(2)}, u32[]{:S(2)}) collective-permute-start(bf16[8,4096]{1,0:T(8,128)(2,1)S(1)} %get-tuple-element.194), channel_id=1, source_target_pairs={{0,64},{2,66},{64,0},{66,2},{1,65},{3,67},{65,1},{67,3},{4,68},{6,... | collective-permute-start | bytes 196616 | tf_op jit(solution)/shard_map/ppermute | solution.py:91
  454.4 22.4 %collective-permute-start.52 = (bf16[128,2048]{1,0:T(8,128)(2,1)S(1)}, bf16[128,2048]{1,0:T(8,128)(2,1)S(1)}, u32[]{:S(2)}, u32[]{:S(2)}) collective-permute-start(bf16[128,2048]{1,0:T(8,128)(2,1)S(1)} %get-tuple-element.147), channel_id=1, source_target_pairs={{0,64},{2,66},{64,0},{66,2},{1,65},{3,67},{65,1},{67,3},{4,68},{6,... | collective-permute-start | bytes 1572872 | tf_op jit(solution)/shard_map/ppermute | solution.py:91
  464.6 15.1 %collective-permute-start.60 = (bf16[8,4096]{1,0:T(8,128)(2,1)S(1)}, bf16[8,4096]{1,0:T(8,128)(2,1)S(1)}, u32[]{:S(2)}, u32[]{:S(2)}) collective-permute-start(bf16[8,4096]{1,0:T(8,128)(2,1)S(1)} %get-tuple-element.193), channel_id=1, source_target_pairs={{0,66},{2,0},{64,2},{66,64},{1,67},{3,1},{65,3},{67,65},{4,70},{6,... | collective-permute-start | bytes 196616 | tf_op jit(solution)/shard_map/ppermute | solution.py:91
  (141 other events, 1439.7 us)
Sparse Core Ops, SparseCore 0:
  21.0 65.0 all-gather.4
  89.2 86.5 all-gather.6
  177.9 51.2 all-gather.8
  291.9 92.9 reduce-scatter.2
  392.8 81.5 reduce-scatter.4
where the time goes:
time: 514 us; the launch traced here: 504 us
  waiting for transfers between devices  166 us (32%)
  starting transfers between devices  104 us (20%)
  Pallas kernels  94 us (18%)
  local copies, waits for them, and re-layouts  68.3 us (13%)
  other arithmetic  30.2 us (6%)
  between operations  21.4 us (4%)
  blocking collectives  15.3 us (3%)
  matrix products  5.8 us (1%)
    ppermute x33, waiting for transfers between devices, px(): return lax.ppermute(value, RING, [(i, (i + step) % 4) for i in range(4)])  123 us
    pallas_call x29, Pallas kernels, kernel(): pl.pallas_call(outer, out_shape=outs, compiler_params=pltpu.CompilerParam...  94 us
    unnamed x206, local copies, waits for them, and re-layouts  48.2 us
    ppermute x33, starting transfers between devices, px(): return lax.ppermute(value, RING, [(i, (i + step) % 4) for i in range(4)])  42.1 us
    ppermute x32, starting transfers between devices, swap(): return lax.ppermute(value, axis, [(0, 1), (1, 0)])  41.1 us
    ppermute x32, waiting for transfers between devices, swap(): return lax.ppermute(value, axis, [(0, 1), (1, 0)])  31.3 us
    all_gather x1, blocking collectives, per_device(): caption = lax.all_gather(caption, ('xh', 'xl', 'c'), axis=0, tiled=True)  15.3 us
  transfers between devices with their start and end apart: 73, of which 29 were waited for; matrix products, arithmetic and copies ran while one was open for 10% of the time, Pallas kernels for 19%

commit v1 on v0

--- a/solution.py
+++ b/solution.py
@@ -526,7 +526,9 @@
     def exchange(weights):
         pairs = [halves(w) for w in weights]
         mine = jnp.concatenate([p[0] for p in pairs], 1)
-        theirs = swap(jnp.concatenate([p[1] for p in pairs], 1), "xh")
+        return mine, swap(jnp.concatenate([p[1] for p in pairs], 1), "xh")
+
+    def both_of(mine, theirs):
         return jnp.stack(in_order(mine, theirs), 0)
 
     def home(first, second):
@@ -537,7 +539,7 @@
     def join(keep, theirs):
         return jnp.concatenate(in_order(keep, theirs), 1)
 
-    pair = exchange(
+    pair = both_of(*exchange(
         (
             gained(self_query, gain_one),
             gained(self_key, gain_one),
@@ -546,21 +548,11 @@
             gained(cross_query, gain_two),
             cross_output.T,
         )
-    )
+    ))
     first = lax.all_gather(pair.reshape(128, 1536), PLANE, axis=0, tiled=True)
-    resid = mix_features(image_tokens[0])
-    normed_one, _ = stats(resid.astype(F32))
-    grad_low = mix_features(output_grad[0])
-    tokens = after(jnp.concatenate([normed_one.astype(BF), grad_low], 0), pair)
-    pieces = [tokens, px(tokens, 1), px(tokens, -1)]
-    caption = after(after(caption_embed[0], pieces[1]), pieces[2])
-    caption = lax.all_gather(caption, ("xh", "xl", "c"), axis=0, tiled=True)
-    caption = caption.reshape(64, 2, 16, 128).transpose(2, 0, 1, 3).reshape(16, 64, 256)
-    pieces.append(jnp.concatenate(far_of(pieces[1], pieces[2]), 0))
-    tokens = [side for piece in pieces for side in (piece, swap(piece, "c"))]
-    pair_late = exchange(
+    mine_late, theirs_late = exchange(
         (
-            after(gained(up_weight, gain_three), caption),
+            gained(up_weight, gain_three),
             down_weight.T,
             cross_key[:64],
             cross_value[:64],
@@ -568,23 +560,34 @@
             cross_value[64:],
         )
     )
-    pair_kv = jnp.stack([pair_late[:, :, 2048:2560], pair_late[:, :, 2560:]], 1)
-    pair_kv = pair_kv.reshape(256, 512)
-    feed_weight = pair_late[:, :, :2048].reshape(128, 2048)
-    feed_weight = lax.all_gather(feed_weight, PLANE, axis=0, tiled=True)
+    resid = mix_features(image_tokens[0])
+    normed_one, _ = stats(resid.astype(F32))
+    grad_low = mix_features(output_grad[0])
+    caption = after(caption_embed[0], pair)
+    caption = lax.all_gather(caption, ("xh", "xl", "c"), axis=0, tiled=True)
+    caption = caption.reshape(64, 2, 16, 128).transpose(2, 0, 1, 3).reshape(16, 64, 256)
+    tokens = after(jnp.concatenate([normed_one.astype(BF), grad_low], 0), caption)
+    pieces = [tokens, px(tokens, 1), px(tokens, -1)]
     caption = lax.all_to_all(caption, PLANE, split_axis=0, concat_axis=0, tiled=True)
     caption = caption.reshape(1024, 256)
-    kv = dot(caption, pair_kv, 1, 0, BF).reshape(16, 64, 512)
-    kv = lax.all_to_all(kv, PLANE, split_axis=0, concat_axis=0, tiled=True)
+    across = far_of(after(pieces[1], caption), after(pieces[2], caption))
+    pieces.append(jnp.concatenate(across, 0))
+    tokens = [side for piece in pieces for side in (piece, swap(piece, "c"))]
+    pair_kv = both_of(mine_late[:, 2048:], theirs_late[:, 2048:])
+    pair_kv = jnp.stack([pair_kv[:, :, :512], pair_kv[:, :, 512:]], 1).reshape(256, 512)
+    kv = dot(caption, pair_kv, 1, 0, BF)
+    pair_late = both_of(mine_late[:, :2048], hold(theirs_late, [*across, kv])[:, :2048])
+    feed_weight = pair_late.reshape(128, 2048)
+    feed_weight = lax.all_gather(feed_weight, PLANE, axis=0, tiled=True)
+    kv = lax.all_to_all(kv.reshape(16, 64, 512), PLANE, split_axis=0, concat_axis=0, tiled=True)
     qkv, p1, o1, keep, send = attend(0, 4, tokens, first)
     kv, both = fold(place, kv.reshape(16, 64, 512), first, [keep])
     kv_weight = lax.all_gather(after(pair_kv, kv), PLANE, axis=0, tiled=True)
-    parts, low = reduce_tokens(keep, swap(send, "c"))
-    both = hold(both, parts[2:4])
     slots_come = [px(both[1], -1), px(both[2], 1), px(both[3], 2)]
     slots = jnp.stack([both[0], *slots_come], 0)
     slots = (slots, swap(slots, "c"))
 
+    parts, _ = reduce_tokens(keep, swap(send, "c"))
     length = jnp.where(xl == 0, caption_lengths[0, 0], caption_lengths[0, 1])[None]
     n2, i2, p2, x3, n3, i3 = middle(length, resid, parts, slots)
 
@@ -658,7 +661,7 @@
         keeps.append(keep)
         others.append(swap(send, "c"))
     parts, low = reduce_tokens(keeps, others)
-    cross_grad, grad_kv = unfold(place, slot_back, kv, first)
+    cross_grad, grad_kv = unfold(place, slot_back, kv, first, keeps[-1:])
     more = more_grad(*back, o1, cross_grad, tokens, keeps[-1:])
     kv_all = lax.all_to_all(
         jnp.broadcast_to(grad_kv[None], (16, 64, 512)),

time: 514 us -> 492 us (0.957)
  the two profiles are of different devices: /device:TPU:1 before, /device:TPU:25 now
where the time goes in v1:
time: 492 us; the launch traced here: 483 us
  waiting for transfers between devices  141 us (29%)
  starting transfers between devices  119 us (24%)
  Pallas kernels  91.8 us (19%)
  local copies, waits for them, and re-layouts  60.9 us (12%)
  other arithmetic  31.1 us (6%)
  between operations  20.8 us (4%)
  blocking collectives  14.8 us (3%)
    ppermute x33, waiting for transfers between devices, px(): return lax.ppermute(value, RING, [(i, (i + step) % 4) for i in range(4)])  104 us
    pallas_call x29, Pallas kernels, kernel(): pl.pallas_call(outer, out_shape=outs, compiler_params=pltpu.CompilerParam...  91.8 us
    ppermute x33, starting transfers between devices, px(): return lax.ppermute(value, RING, [(i, (i + step) % 4) for i in range(4)])  54.2 us
    ppermute x32, starting transfers between devices, swap(): return lax.ppermute(value, axis, [(0, 1), (1, 0)])  45.2 us
    unnamed x184, local copies, waits for them, and re-layouts  43.8 us
    ppermute x32, waiting for transfers between devices, swap(): return lax.ppermute(value, axis, [(0, 1), (1, 0)])  22.4 us
    all_gather x1, blocking collectives, per_device(): caption = lax.all_gather(caption, ('xh', 'xl', 'c'), axis=0, tiled=True)  14.8 us
  transfers between devices with their start and end apart: 73, of which 32 were waited for; matrix products, arithmetic and copies ran while one was open for 10% of the time, Pallas kernels for 19%

profile of v1, /device:TPU:25, one launch (start us, length us, event | category | flops | bytes accessed | tf_op | source)
XLA Modules:
  0.0 482.7 jit_solution(9430714877432240286)
XLA Ops:
  15.1 4.5 collective-permute-done
  23.9 14.8 %all-gather = bf16[1,64,4096]{2,1,0:T(8,128)(2,1)S(1)} all-gather(bf16[1,8,4096]{2,1,0:T(8,128)(2,1)S(1)} %add_convert_fusion.20), channel_id=2, replica_groups=mesh['xh'=2,'y'=4,'z'=4,'xl'=2,'c'=2] {'xh','xl','c'}, dimensions={1}, use_global_device_ids=true | all-gather | bytes 589824 | tf_op jit(solution)/shard_map/all_gather | solution.py:567
  45.7 7.6 %all-to-all-start = ((bf16[16,64,256]{2,1,0:T(8,128)(2,1)}), bf16[16,64,256]{2,1,0:T(8,128)(2,1)S(1)}, u32[]{:S(2)}, u32[]{:S(2)}) async-start(bf16[16,64,256]{2,1,0:T(8,128)(2,1)} %reshape.168), calls=%async_computation | async-start | bytes 1048576 | tf_op jit(solution)/shard_map/all_to_all | solution.py:571
  56.7 7.6 %all-to-all-done = bf16[16,64,256]{2,1,0:T(8,128)(2,1)S(1)} async-done(((bf16[16,64,256]{2,1,0:T(8,128)(2,1)}), bf16[16,64,256]{2,1,0:T(8,128)(2,1)S(1)}, u32[]{:S(2)}, u32[]{:S(2)}) %all-to-all-start) | async-done | bytes 524320 | tf_op jit(solution)/shard_map/all_to_all | solution.py:571
  67.8 11.3 %collective-permute-start.7 = (bf16[128,2048]{1,0:T(8,128)(2,1)S(1)}, bf16[128,2048]{1,0:T(8,128)(2,1)S(1)}, u32[]{:S(2)}, u32[]{:S(2)}) collective-permute-start(bf16[128,2048]{1,0:T(8,128)(2,1)S(1)} %add_convert_fusion.15), channel_id=1, source_target_pairs={{0,66},{2,0},{64,2},{66,64},{1,67},{3,1},{65,3},{67,65},{4,70},{6,... | collective-permute-start | bytes 1572872 | tf_op jit(solution)/shard_map/ppermute | solution.py:91
  80.6 5.1 %collective-permute-done.13.refs_0_ = bf16[64,3072]{1,0:T(8,128)(2,1)S(1)} collective-permute-done((bf16[64,3072]{1,0:T(8,128)(2,1)}, bf16[64,3072]{1,0:T(8,128)(2,1)S(1)}, u32[]{:S(2)}, u32[]{:S(2)}) %collective-permute-start.13) | collective-permute-done | bytes 393248 | tf_op jit(solution)/shard_map/ppermute | solution.py:99
  89.2 4.4 collective-permute-done.6.refs_1_
  94.6 8.0 %collective-permute-start.1 = (bf16[256,2048]{1,0:T(8,128)(2,1)S(1)}, bf16[256,2048]{1,0:T(8,128)(2,1)}, u32[]{:S(2)}, u32[]{:S(2)}) collective-permute-start(bf16[256,2048]{1,0:T(8,128)(2,1)S(1)} %add_convert_fusion.2.refs_0_.ga.refs_3_.refs_4_), channel_id=1, source_target_pairs={{0,1},{1,0},{2,3},{3,2},{4,5},{5,4},{6,7},{7,6},{8,9},{9,8},{10,11... | collective-permute-start | bytes 3145736 | tf_op jit(solution)/shard_map/ppermute | solution.py:99
  105.4 6.7 %all-to-all-start.1 = ((bf16[16,64,512]{2,1,0:T(8,128)(2,1)}), bf16[16,64,512]{2,1,0:T(8,128)(2,1)}, u32[]{:S(2)}, u32[]{:S(2)}) async-start(bf16[16,64,512]{2,1,0:T(8,128)(2,1)} %bitcast.141), calls=%async_computation.1 | async-start | bytes 2097152 | tf_op jit(solution)/shard_map/all_to_all | solution.py:582
  115.3 12.3 %attend.1 = (bf16[1024,768]{1,0:T(8,128)(2,1)S(1)}, bf16[4,2,256,256]{3,2,1,0:T(8,128)(2,1)S(1)}, bf16[1024,256]{1,0:T(8,128)(2,1)S(1)}, bf16[4,128,2048]{2,1,0:T(8,128)(2,1)S(1)}, bf16[4,128,2048]{2,1,0:T(8,128)(2,1)}) custom-call(bf16[256,2048]{1,0:T(8,128)(2,1)S(1)} %add_convert_fusion.2.refs_0_.ga.refs_3_.refs_4_, ...), custom_call_target="tpu_custom_call" | custom-call | flops 1000 | bytes 1000 | tf_op jit(solution)/shard_map/attend/pallas_call | solution.py:58
  147.8 4.9 %collective-permute-done.14 = bf16[64,2048]{1,0:T(8,128)(2,1)} collective-permute-done((bf16[64,2048]{1,0:T(8,128)(2,1)}, bf16[64,2048]{1,0:T(8,128)(2,1)}, u32[]{:S(2)}, u32[]{:S(2)}) %collective-permute-start.14) | collective-permute-done | bytes 262176 | tf_op jit(solution)/shard_map/ppermute | solution.py:91
  152.7 6.8 %collective-permute-done.15 = bf16[64,2048]{1,0:T(8,128)(2,1)} collective-permute-done((bf16[64,2048]{1,0:T(8,128)(2,1)}, bf16[64,2048]{1,0:T(8,128)(2,1)}, u32[]{:S(2)}, u32[]{:S(2)}) %collective-permute-start.15) | collective-permute-done | bytes 262176 | tf_op jit(solution)/shard_map/ppermute | solution.py:91
  168.3 8.8 %collective-permute-done.10.refs_3_ = bf16[128,2048]{1,0:T(8,128)(2,1)S(1)} collective-permute-done((bf16[128,2048]{1,0:T(8,128)(2,1)S(1)}, bf16[128,2048]{1,0:T(8,128)(2,1)S(1)}, u32[]{:S(2)}, u32[]{:S(2)}) %collective-permute-start.10) | collective-permute-done | bytes 524320 | tf_op jit(solution)/shard_map/ppermute | solution.py:91
  179.7 9.9 %collective-permute-done.12.refs_5_ = bf16[128,2048]{1,0:T(8,128)(2,1)S(1)} collective-permute-done((bf16[128,2048]{1,0:T(8,128)(2,1)S(1)}, bf16[128,2048]{1,0:T(8,128)(2,1)S(1)}, u32[]{:S(2)}, u32[]{:S(2)}) %collective-permute-start.12) | collective-permute-done | bytes 524320 | tf_op jit(solution)/shard_map/ppermute | solution.py:91
  204.2 5.3 %feed.4 = (bf16[1024,1024]{1,0:T(8,128)(2,1)S(1)}, bf16[1024,1024]{1,0:T(8,128)(2,1)S(1)}, bf16[1024,2048]{1,0:T(8,128)(2,1)S(1)}, bf16[128,2048]{1,0:T(8,128)(2,1)S(1)}, bf16[128,2048]{1,0:T(8,128)(2,1)S(1)}) custom-call(bf16[128,2048]{1,0:T(8,128)(2,1)} %get-tuple-element.77.xa.refs_11_, bf16[128,2048]{1,0:T(8,128)(2,1)S(1)} %copy-done.61, ...), custom_call_target="tpu_custom_call" | custom-call | flops 1000 | bytes 1000 | tf_op jit(solution)/shard_map/feed/pallas_call | solution.py:58
  217.5 5.5 %feed.5 = (bf16[1024,1024]{1,0:T(8,128)(2,1)S(1)}, bf16[1024,1024]{1,0:T(8,128)(2,1)S(1)}, bf16[1024,2048]{1,0:T(8,128)(2,1)S(1)}, bf16[128,2048]{1,0:T(8,128)(2,1)S(1)}, bf16[128,2048]{1,0:T(8,128)(2,1)S(1)}) custom-call(bf16[128,2048]{1,0:T(8,128)(2,1)} %hold.13.xa, ...), custom_call_target="tpu_custom_call", output_to_operand_aliasing={{0}: (5, {}), {1}: (6, {}), {2}: (7, {})} | custom-call | flops 1000 | bytes 1000 | tf_op jit(solution)/shard_map/feed/pallas_call | solution.py:58
  224.6 5.3 %feed.6 = (bf16[1024,1024]{1,0:T(8,128)(2,1)S(1)}, bf16[1024,1024]{1,0:T(8,128)(2,1)S(1)}, bf16[1024,2048]{1,0:T(8,128)(2,1)S(1)}, bf16[128,2048]{1,0:T(8,128)(2,1)S(1)}, bf16[128,2048]{1,0:T(8,128)(2,1)S(1)}) custom-call(bf16[128,2048]{1,0:T(8,128)(2,1)} %hold.15.refs_0_, ...), custom_call_target="tpu_custom_call", output_to_operand_aliasing={{0}: (5, {}), {1}: (6, {}), {2}: (7, {})} | custom-call | flops 1000 | bytes 1000 | tf_op jit(solution)/shard_map/feed/pallas_call | solution.py:58
  230.5 5.0 %feed.7 = (bf16[1024,1024]{1,0:T(8,128)(2,1)S(1)}, bf16[1024,1024]{1,0:T(8,128)(2,1)S(1)}, bf16[1024,2048]{1,0:T(8,128)(2,1)S(1)}, bf16[128,2048]{1,0:T(8,128)(2,1)S(1)}, bf16[128,2048]{1,0:T(8,128)(2,1)S(1)}) custom-call(bf16[128,2048]{1,0:T(8,128)(2,1)S(1)} %pad_maximum_fusion.2.refs_0_, ...), custom_call_target="tpu_custom_call", output_to_operand_aliasing={{0}: (5, {}), {1}: (6, {}), {2}: (7, {})} | custom-call | flops 1000 | bytes 1000 | tf_op jit(solution)/shard_map/feed/pallas_call | solution.py:58
  246.6 13.0 %feed_grad.1.refs_0_ = bf16[2048,2048]{1,0:T(8,128)(2,1)} custom-call(bf16[1024,2048]{1,0:T(8,128)(2,1)S(1)} %copy-done.4, bf16[1024,1024]{1,0:T(8,128)(2,1)S(1)} %copy-done.9, bf16[1024,1024]{1,0:T(8,128)(2,1)S(1)} %get-tuple-element.91.refs_2_.refs_0_, bf16[256,2048]{1,0:T(8,128)(2,1)} %copy-done.10, ...), custom_call_target="tpu_custom_call" | custom-call | flops 1000 | bytes 1000 | tf_op jit(solution)/shard_map/feed_grad/pallas_call | solution.py:58
  268.9 4.3 middle_back.1
  280.3 9.0 %collective-permute-done.33.refs_0_ = bf16[128,2048]{1,0:T(8,128)(2,1)S(1)} collective-permute-done((bf16[128,2048]{1,0:T(8,128)(2,1)S(1)}, bf16[128,2048]{1,0:T(8,128)(2,1)S(1)}, u32[]{:S(2)}, u32[]{:S(2)}) %collective-permute-start.33) | collective-permute-done | bytes 524320 | tf_op jit(solution)/shard_map/ppermute | solution.py:91
  309.9 4.6 collective-permute-done.45.refs_9_.refs_3_
  319.2 4.3 unfold.1
  326.0 4.7 all-to-all-start.2
  337.6 9.9 %more_grad.1.refs_0_ = bf16[2048,1536]{1,0:T(8,128)(2,1)} custom-call(bf16[1024,768]{1,0:T(8,128)(2,1)S(1)} %get-tuple-element.118.refs_0_, bf16[1024,2048]{1,0:T(8,128)(2,1)S(1)} %copy-done.6, bf16[1024,256]{1,0:T(8,128)(2,1)S(1)} %copy-done.53, bf16[2048,512]{1,0:T(8,128)(2,1)S(1)} %copy-done.34, bf16[256,2048]{1,0:T(8,128)(2,1)} %copy-done.10, ...), custom_call_target="tpu_custom_call" | custom-call | flops 1000 | bytes 1000 | tf_op jit(solution)/shard_map/more_grad/pallas_call | solution.py:58
  359.8 5.1 %collective-permute-start.54 = (bf16[128,2048]{1,0:T(8,128)(2,1)}, bf16[128,2048]{1,0:T(8,128)(2,1)S(1)}, u32[]{:S(2)}, u32[]{:S(2)}) collective-permute-start(bf16[128,2048]{1,0:T(8,128)(2,1)} %copy-done.62), channel_id=1, source_target_pairs={{0,1},{1,0},{2,3},{3,2},{4,5},{5,4},{6,7},{7,6},{8,9},{9,8},{10,11... | collective-permute-start | bytes 1572872 | tf_op jit(solution)/shard_map/ppermute | solution.py:99
  373.0 9.2 %collective-permute-done.55.refs_4_ = bf16[128,2048]{1,0:T(8,128)(2,1)S(1)} collective-permute-done((bf16[128,2048]{1,0:T(8,128)(2,1)}, bf16[128,2048]{1,0:T(8,128)(2,1)S(1)}, u32[]{:S(2)}, u32[]{:S(2)}) %collective-permute-start.55) | collective-permute-done | bytes 524320 | tf_op jit(solution)/shard_map/ppermute | solution.py:91
  382.6 10.8 %collective-permute-done.56.refs_5_ = bf16[128,2048]{1,0:T(8,128)(2,1)S(1)} collective-permute-done((bf16[128,2048]{1,0:T(8,128)(2,1)S(1)}, bf16[128,2048]{1,0:T(8,128)(2,1)S(1)}, u32[]{:S(2)}, u32[]{:S(2)}) %collective-permute-start.56) | collective-permute-done | bytes 524320 | tf_op jit(solution)/shard_map/ppermute | solution.py:91
  401.2 10.3 %feed_out.1 = (bf16[4,128,2048]{2,1,0:T(8,128)(2,1)}, bf16[4,128,2048]{2,1,0:T(8,128)(2,1)}) custom-call(bf16[1024,1024]{1,0:T(8,128)(2,1)} %copy-done.7, bf16[2048,2048]{1,0:T(8,128)(2,1)} %all-gather.7.cloned.1.call-done.w_ref.refs_4_.refs_1_, bf16[2048,1536]{1,0:T(8,128)(2,1)} %hold.22.refs_2_), custom_call_target="tpu_custom_call" | custom-call | flops 1000 | bytes 1000 | tf_op jit(solution)/shard_map/feed_out/pallas_call | solution.py:58
  433.6 7.9 %collective-permute-done.50.refs_1_ = bf16[128,2048]{1,0:T(8,128)(2,1)S(1)} collective-permute-done((bf16[128,2048]{1,0:T(8,128)(2,1)S(1)}, bf16[128,2048]{1,0:T(8,128)(2,1)S(1)}, u32[]{:S(2)}, u32[]{:S(2)}) %collective-permute-start.50) | collective-permute-done | bytes 524320 | tf_op jit(solution)/shard_map/ppermute | solution.py:91
  445.4 7.4 %collective-permute-done.52.refs_3_ = bf16[128,2048]{1,0:T(8,128)(2,1)S(1)} collective-permute-done((bf16[128,2048]{1,0:T(8,128)(2,1)S(1)}, bf16[128,2048]{1,0:T(8,128)(2,1)S(1)}, u32[]{:S(2)}, u32[]{:S(2)}) %collective-permute-start.52) | collective-permute-done | bytes 524320 | tf_op jit(solution)/shard_map/ppermute | solution.py:91
  465.2 9.3 %collective-permute-start.64 = (f32[3,64]{1,0:T(4,128)S(1)}, f32[3,64]{1,0:T(4,128)S(1)}, u32[]{:S(2)}, u32[]{:S(2)}) collective-permute-start(f32[3,64]{1,0:T(4,128)S(1)} %fusion.33), channel_id=1, source_target_pairs={{0,1},{1,0},{2,3},{3,2},{4,5},{5,4},{6,7},{7,6},{8,9},{9,8},{10,11... | collective-permute-start | bytes 2312 | tf_op jit(solution)/shard_map/ppermute | solution.py:99
  (441 shorter events, 218.2 us)
Async XLA Ops:
  7.2 105.3 %all-gather.5.cloned.1.call-start = ((), (), s32[]{:S(2)}) async-start(), calls=%async_computation.5 | async-start | bytes 6684672 | tf_op jit(solution)/shard_map/all_gather | solution.py:552
  42.6 25.0 %collective-permute-start.4 = (bf16[256,2048]{1,0:T(8,128)(2,1)S(1)}, bf16[256,2048]{1,0:T(8,128)(2,1)S(1)}, u32[]{:S(2)}, u32[]{:S(2)}) collective-permute-start(bf16[256,2048]{1,0:T(8,128)(2,1)S(1)} %add_convert_fusion.2.refs_0_.ga.refs_3_.refs_4_), channel_id=1, source_target_pairs={{0,66},{2,0},{64,2},{66,64},{1,67},{3,1},{65,3},{67,65},{4,70},{6,... | collective-permute-start | bytes 3145736 | tf_op jit(solution)/shard_map/ppermute | solution.py:91
  45.7 18.6 %all-to-all-start = ((bf16[16,64,256]{2,1,0:T(8,128)(2,1)}), bf16[16,64,256]{2,1,0:T(8,128)(2,1)S(1)}, u32[]{:S(2)}, u32[]{:S(2)}) async-start(bf16[16,64,256]{2,1,0:T(8,128)(2,1)} %reshape.168), calls=%async_computation | async-start | bytes 1048576 | tf_op jit(solution)/shard_map/all_to_all | solution.py:571
  53.3 146.5 %all-gather.7.cloned.1.call-start = ((), (), s32[]{:S(2)}) async-start(), calls=%async_computation.6 | async-start | bytes 8912896 | tf_op jit(solution)/shard_map/all_gather | solution.py:581
  53.3 26.0 %collective-permute-start.2 = (bf16[256,2048]{1,0:T(8,128)(2,1)S(1)}, bf16[256,2048]{1,0:T(8,128)(2,1)}, u32[]{:S(2)}, u32[]{:S(2)}) collective-permute-start(bf16[256,2048]{1,0:T(8,128)(2,1)S(1)} %add_convert_fusion.2.refs_0_.ga.refs_3_.refs_4_), channel_id=1, source_target_pairs={{0,2},{2,64},{64,66},{66,0},{1,3},{3,65},{65,67},{67,1},{4,6},{6,6... | collective-permute-start | bytes 3145736 | tf_op jit(solution)/shard_map/ppermute | solution.py:91
  55.3 30.4 %collective-permute-start.13 = (bf16[64,3072]{1,0:T(8,128)(2,1)}, bf16[64,3072]{1,0:T(8,128)(2,1)S(1)}, u32[]{:S(2)}, u32[]{:S(2)}) collective-permute-start(bf16[64,3072]{1,0:T(8,128)(2,1)} %constant_dynamic-update-slice_fusion.14), channel_id=1, source_target_pairs={{0,64},{64,0},{1,65},{65,1},{2,66},{66,2},{3,67},{67,3},{4,68},{68... | collective-permute-start | bytes 1179656 | tf_op jit(solution)/shard_map/ppermute | solution.py:99
  67.8 21.4 %collective-permute-start.7 = (bf16[128,2048]{1,0:T(8,128)(2,1)S(1)}, bf16[128,2048]{1,0:T(8,128)(2,1)S(1)}, u32[]{:S(2)}, u32[]{:S(2)}) collective-permute-start(bf16[128,2048]{1,0:T(8,128)(2,1)S(1)} %add_convert_fusion.15), channel_id=1, source_target_pairs={{0,66},{2,0},{64,2},{66,64},{1,67},{3,1},{65,3},{67,65},{4,70},{6,... | collective-permute-start | bytes 1572872 | tf_op jit(solution)/shard_map/ppermute | solution.py:91
  94.6 17.9 %collective-permute-start.1 = (bf16[256,2048]{1,0:T(8,128)(2,1)S(1)}, bf16[256,2048]{1,0:T(8,128)(2,1)}, u32[]{:S(2)}, u32[]{:S(2)}) collective-permute-start(bf16[256,2048]{1,0:T(8,128)(2,1)S(1)} %add_convert_fusion.2.refs_0_.ga.refs_3_.refs_4_), channel_id=1, source_target_pairs={{0,1},{1,0},{2,3},{3,2},{4,5},{5,4},{6,7},{7,6},{8,9},{9,8},{10,11... | collective-permute-start | bytes 3145736 | tf_op jit(solution)/shard_map/ppermute | solution.py:99
  105.4 29.5 %all-to-all-start.1 = ((bf16[16,64,512]{2,1,0:T(8,128)(2,1)}), bf16[16,64,512]{2,1,0:T(8,128)(2,1)}, u32[]{:S(2)}, u32[]{:S(2)}) async-start(bf16[16,64,512]{2,1,0:T(8,128)(2,1)} %bitcast.141), calls=%async_computation.1 | async-start | bytes 2097152 | tf_op jit(solution)/shard_map/all_to_all | solution.py:582
  112.1 130.7 %all-gather.9.cloned.1.call-start = ((), (), s32[]{:S(2)}) async-start(), calls=%async_computation.7 | async-start | bytes 4456448 | tf_op jit(solution)/shard_map/all_gather | solution.py:585
  140.7 218.0 %reduce-scatter.3.cloned.1.call-start = ((), (), s32[]{:S(2)}) async-start(), calls=%async_computation.8 | async-start | bytes 8912896 | tf_op jit(solution)/shard_map/reduce_scatter | solution.py:628
  140.7 21.0 %collective-permute-start.9 = (bf16[4,128,2048]{2,1,0:T(8,128)(2,1)}, bf16[4,128,2048]{2,1,0:T(8,128)(2,1)}, u32[]{:S(2)}, u32[]{:S(2)}) collective-permute-start(bf16[4,128,2048]{2,1,0:T(8,128)(2,1)} %get-tuple-element.74), channel_id=1, source_target_pairs={{0,1},{1,0},{2,3},{3,2},{4,5},{5,4},{6,7},{7,6},{8,9},{9,8},{10,11... | collective-permute-start | bytes 6291464 | tf_op jit(solution)/shard_map/ppermute | solution.py:99
  144.4 15.1 %collective-permute-start.15 = (bf16[64,2048]{1,0:T(8,128)(2,1)}, bf16[64,2048]{1,0:T(8,128)(2,1)}, u32[]{:S(2)}, u32[]{:S(2)}) collective-permute-start(bf16[64,2048]{1,0:T(8,128)(2,1)} %get-tuple-element.162), channel_id=1, source_target_pairs={{0,2},{2,64},{64,66},{66,0},{1,3},{3,65},{65,67},{67,1},{4,6},{6,6... | collective-permute-start | bytes 786440 | tf_op jit(solution)/shard_map/ppermute | solution.py:91
  165.0 14.7 %collective-permute-start.11 = (bf16[128,2048]{1,0:T(8,128)(2,1)S(1)}, bf16[128,2048]{1,0:T(8,128)(2,1)S(1)}, u32[]{:S(2)}, u32[]{:S(2)}) collective-permute-start(bf16[128,2048]{1,0:T(8,128)(2,1)S(1)} %get-tuple-element.150), channel_id=1, source_target_pairs={{0,2},{2,64},{64,66},{66,0},{1,3},{3,65},{65,67},{67,1},{4,6},{6,6... | collective-permute-start | bytes 1572872 | tf_op jit(solution)/shard_map/ppermute | solution.py:91
  165.3 24.3 %collective-permute-start.12 = (bf16[128,2048]{1,0:T(8,128)(2,1)S(1)}, bf16[128,2048]{1,0:T(8,128)(2,1)S(1)}, u32[]{:S(2)}, u32[]{:S(2)}) collective-permute-start(bf16[128,2048]{1,0:T(8,128)(2,1)S(1)} %get-tuple-element.149), channel_id=1, source_target_pairs={{0,64},{2,66},{64,0},{66,2},{1,65},{3,67},{65,1},{67,3},{4,68},{6,... | collective-permute-start | bytes 1572872 | tf_op jit(solution)/shard_map/ppermute | solution.py:91
  196.3 15.1 %collective-permute-start.18 = (bf16[128,2048]{1,0:T(8,128)(2,1)}, bf16[128,2048]{1,0:T(8,128)(2,1)}, u32[]{:S(2)}, u32[]{:S(2)}) collective-permute-start(bf16[128,2048]{1,0:T(8,128)(2,1)} %get-tuple-element.77.xa.refs_11_), channel_id=1, source_target_pairs={{0,2},{2,64},{64,66},{66,0},{1,3},{3,65},{65,67},{67,1},{4,6},{6,6... | collective-permute-start | bytes 1572872 | tf_op jit(solution)/shard_map/ppermute | solution.py:91
  196.3 15.9 %collective-permute-start.22 = (bf16[128,2048]{1,0:T(8,128)(2,1)}, bf16[128,2048]{1,0:T(8,128)(2,1)}, u32[]{:S(2)}, u32[]{:S(2)}) collective-permute-start(bf16[128,2048]{1,0:T(8,128)(2,1)} %get-tuple-element.77.xa.refs_11_), channel_id=1, source_target_pairs={{0,66},{2,0},{64,2},{66,64},{1,67},{3,1},{65,3},{67,65},{4,70},{6,... | collective-permute-start | bytes 1572872 | tf_op jit(solution)/shard_map/ppermute | solution.py:91
  237.0 23.9 %collective-permute-start.30 = (bf16[128,2048]{1,0:T(8,128)(2,1)S(1)}, bf16[128,2048]{1,0:T(8,128)(2,1)}, u32[]{:S(2)}, u32[]{:S(2)}) collective-permute-start(bf16[128,2048]{1,0:T(8,128)(2,1)S(1)} %add_convert_fusion.10.refs_12_), channel_id=1, source_target_pairs={{0,2},{2,64},{64,66},{66,0},{1,3},{3,65},{65,67},{67,1},{4,6},{6,6... | collective-permute-start | bytes 1572872 | tf_op jit(solution)/shard_map/ppermute | solution.py:91
  238.2 22.7 %collective-permute-start.28 = (bf16[128,2048]{1,0:T(8,128)(2,1)S(1)}, bf16[128,2048]{1,0:T(8,128)(2,1)}, u32[]{:S(2)}, u32[]{:S(2)}) collective-permute-start(bf16[128,2048]{1,0:T(8,128)(2,1)S(1)} %add_convert_fusion.11.refs_11_), channel_id=1, source_target_pairs={{0,66},{2,0},{64,2},{66,64},{1,67},{3,1},{65,3},{67,65},{4,70},{6,... | collective-permute-start | bytes 1572872 | tf_op jit(solution)/shard_map/ppermute | solution.py:91
  241.6 23.0 %collective-permute-start.32 = (bf16[128,2048]{1,0:T(8,128)(2,1)}, bf16[128,2048]{1,0:T(8,128)(2,1)}, u32[]{:S(2)}, u32[]{:S(2)}) collective-permute-start(bf16[128,2048]{1,0:T(8,128)(2,1)} %add_convert_fusion.9.refs_13_), channel_id=1, source_target_pairs={{0,64},{2,66},{64,0},{66,2},{1,65},{3,67},{65,1},{67,3},{4,68},{6,... | collective-permute-start | bytes 1572872 | tf_op jit(solution)/shard_map/ppermute | solution.py:91
  274.7 14.7 %collective-permute-start.33 = (bf16[128,2048]{1,0:T(8,128)(2,1)S(1)}, bf16[128,2048]{1,0:T(8,128)(2,1)S(1)}, u32[]{:S(2)}, u32[]{:S(2)}) collective-permute-start(bf16[128,2048]{1,0:T(8,128)(2,1)S(1)} %get-tuple-element.103.ca), channel_id=1, source_target_pairs={{0,2},{2,64},{64,66},{66,0},{1,3},{3,65},{65,67},{67,1},{4,6},{6,6... | collective-permute-start | bytes 1572872 | tf_op jit(solution)/shard_map/ppermute | solution.py:91
  275.7 24.7 %collective-permute-start.43 = (bf16[4,64,2048]{2,1,0:T(8,128)(2,1)S(1)}, bf16[4,64,2048]{2,1,0:T(8,128)(2,1)S(1)}, u32[]{:S(2)}, u32[]{:S(2)}) collective-permute-start(bf16[4,64,2048]{2,1,0:T(8,128)(2,1)S(1)} %get-tuple-element.117), channel_id=1, source_target_pairs={{0,1},{1,0},{2,3},{3,2},{4,5},{5,4},{6,7},{7,6},{8,9},{9,8},{10,11... | collective-permute-start | bytes 3145736 | tf_op jit(solution)/shard_map/ppermute | solution.py:99
  299.5 17.1 %collective-permute-start.39 = (bf16[128,2048]{1,0:T(8,128)(2,1)S(1)}, bf16[128,2048]{1,0:T(8,128)(2,1)S(1)}, u32[]{:S(2)}, u32[]{:S(2)}) collective-permute-start(bf16[128,2048]{1,0:T(8,128)(2,1)S(1)} %pad_maximum_fusion.3.refs_0_), channel_id=1, source_target_pairs={{0,1},{1,0},{2,3},{3,2},{4,5},{5,4},{6,7},{7,6},{8,9},{9,8},{10,11... | collective-permute-start | bytes 1572872 | tf_op jit(solution)/shard_map/ppermute | solution.py:99
  300.4 16.2 %collective-permute-start.42 = (bf16[128,2048]{1,0:T(8,128)(2,1)S(1)}, bf16[128,2048]{1,0:T(8,128)(2,1)S(1)}, u32[]{:S(2)}, u32[]{:S(2)}) collective-permute-start(bf16[128,2048]{1,0:T(8,128)(2,1)S(1)} %get-tuple-element.115), channel_id=1, source_target_pairs={{0,1},{1,0},{2,3},{3,2},{4,5},{5,4},{6,7},{7,6},{8,9},{9,8},{10,11... | collective-permute-start | bytes 1572872 | tf_op jit(solution)/shard_map/ppermute | solution.py:99
  326.0 25.3 %all-to-all-start.2 = ((bf16[16,64,512]{2,1,0:T(8,128)(2,1)}), bf16[16,64,512]{2,1,0:T(8,128)(2,1)}, u32[]{:S(2)}, u32[]{:S(2)}) async-start(bf16[16,64,512]{2,1,0:T(8,128)(2,1)} %broadcast_in_dim.5), calls=%async_computation.3 | async-start | bytes 2097152 | tf_op jit(solution)/shard_map/all_to_all | solution.py:666
  330.7 122.1 %reduce-scatter.5.cloned.1.call-start = ((), (), s32[]{:S(2)}) async-start(), calls=%async_computation.9 | async-start | bytes 6684672 | tf_op jit(solution)/shard_map/reduce_scatter | solution.py:679
  330.7 23.3 %collective-permute-start.48 = (bf16[128,2048]{1,0:T(8,128)(2,1)}, bf16[128,2048]{1,0:T(8,128)(2,1)}, u32[]{:S(2)}, u32[]{:S(2)}) collective-permute-start(bf16[128,2048]{1,0:T(8,128)(2,1)} %copy-done.63), channel_id=1, source_target_pairs={{0,1},{1,0},{2,3},{3,2},{4,5},{5,4},{6,7},{7,6},{8,9},{9,8},{10,11... | collective-permute-start | bytes 1572872 | tf_op jit(solution)/shard_map/ppermute | solution.py:99
  371.2 22.2 %collective-permute-start.56 = (bf16[128,2048]{1,0:T(8,128)(2,1)S(1)}, bf16[128,2048]{1,0:T(8,128)(2,1)S(1)}, u32[]{:S(2)}, u32[]{:S(2)}) collective-permute-start(bf16[128,2048]{1,0:T(8,128)(2,1)S(1)} %copy-done.46), channel_id=1, source_target_pairs={{0,64},{2,66},{64,0},{66,2},{1,65},{3,67},{65,1},{67,3},{4,68},{6,... | collective-permute-start | bytes 1572872 | tf_op jit(solution)/shard_map/ppermute | solution.py:91
  418.5 37.2 %collective-permute-start.58 = (bf16[8,4096]{1,0:T(8,128)(2,1)S(1)}, bf16[8,4096]{1,0:T(8,128)(2,1)S(1)}, u32[]{:S(2)}, u32[]{:S(2)}) collective-permute-start(bf16[8,4096]{1,0:T(8,128)(2,1)S(1)} %get-tuple-element.192), channel_id=1, source_target_pairs={{0,2},{2,64},{64,66},{66,0},{1,3},{3,65},{65,67},{67,1},{4,6},{6,6... | collective-permute-start | bytes 196616 | tf_op jit(solution)/shard_map/ppermute | solution.py:91
  420.9 34.8 %collective-permute-start.59 = (bf16[8,4096]{1,0:T(8,128)(2,1)S(1)}, bf16[8,4096]{1,0:T(8,128)(2,1)S(1)}, u32[]{:S(2)}, u32[]{:S(2)}) collective-permute-start(bf16[8,4096]{1,0:T(8,128)(2,1)S(1)} %get-tuple-element.194), channel_id=1, source_target_pairs={{0,64},{2,66},{64,0},{66,2},{1,65},{3,67},{65,1},{67,3},{4,68},{6,... | collective-permute-start | bytes 196616 | tf_op jit(solution)/shard_map/ppermute | solution.py:91
  430.4 15.0 %collective-permute-start.51 = (bf16[128,2048]{1,0:T(8,128)(2,1)S(1)}, bf16[128,2048]{1,0:T(8,128)(2,1)S(1)}, u32[]{:S(2)}, u32[]{:S(2)}) collective-permute-start(bf16[128,2048]{1,0:T(8,128)(2,1)S(1)} %get-tuple-element.148), channel_id=1, source_target_pairs={{0,2},{2,64},{64,66},{66,0},{1,3},{3,65},{65,67},{67,1},{4,6},{6,6... | collective-permute-start | bytes 1572872 | tf_op jit(solution)/shard_map/ppermute | solution.py:91
  430.4 22.4 %collective-permute-start.52 = (bf16[128,2048]{1,0:T(8,128)(2,1)S(1)}, bf16[128,2048]{1,0:T(8,128)(2,1)S(1)}, u32[]{:S(2)}, u32[]{:S(2)}) collective-permute-start(bf16[128,2048]{1,0:T(8,128)(2,1)S(1)} %get-tuple-element.147), channel_id=1, source_target_pairs={{0,64},{2,66},{64,0},{66,2},{1,65},{3,67},{65,1},{67,3},{4,68},{6,... | collective-permute-start | bytes 1572872 | tf_op jit(solution)/shard_map/ppermute | solution.py:91
  (130 other events, 1132.6 us)
Sparse Core Ops, SparseCore 0:
  20.6 67.9 all-gather.4
  94.7 84.3 all-gather.6
  181.2 51.2 all-gather.8
  264.8 91.5 reduce-scatter.2
  359.9 81.5 reduce-scatter.4
